TPU v7x, 512 devices: a whole 4x4x16 slice. The times are simulated.
512 devices in a mesh: tm: 32 (over z_lo, y), space: 16 (over z_hi, x, core).
Axes of the slice: x: 4, y: 4, z: 16 (z_hi: 2, z_lo: 8; z = z_hi * 8 + z_lo), core: 2. Of those that a mesh axis runs over, the one named last changes fastest.
Arguments:
- u_nodes: float32 [32, 3, 3, 64, 8, 128], P('tm', None, None, 'space'), may hold values from -4 to 4
Outputs:
- new_nodes: float32 [32, 3, 3, 64, 8, 128], P('tm', None, None, 'space')
All inputs are finite; a program needn't handle non-finite values.
Results may differ from a plain program's by a relative error of at most 0.0003.
Values sent between devices are 32-bit elements; how exact they have to be, the bound alone decides.
No kernel may reach another device: no remote copies, remote signals or barrier semaphores. Data moves between devices by JAX's collectives and lax.ppermute only.
A program may use at most 64 MiB of HBM per device.

v0:
```python
import jax
import jax.numpy as jnp
from jax import lax
from jax.sharding import PartitionSpec as P

STEP = 0.2
VISCOSITY = 0.1
FIRST_ROW = (5.0 / 24.0, 1.0 / 3.0, -1.0 / 24.0)
SECOND_ROW = (-1.0 / 24.0, 1.0 / 3.0, 5.0 / 24.0)


def with_halo(cells, sides, width):
    for axis, dim in sides:
        count = lax.axis_size(axis)
        ends = count - 1
        head = lax.slice_in_dim(cells, 0, width, axis=dim)
        tail = lax.slice_in_dim(cells, cells.shape[dim] - width, cells.shape[dim], axis=dim)
        cells = jnp.concatenate(
            [
                lax.ppermute(tail, axis, [(i, (i + 1) % count) for i in range(ends)]),
                cells,
                lax.ppermute(head, axis, [((i + 1) % count, i) for i in range(ends)]),
            ],
            axis=dim,
        )
    return cells


def passed_along(block, axis, distance):
    devices = range(lax.axis_size(axis))
    route = [(i - distance, i) for i in devices if i - distance in devices]
    return lax.ppermute(block, axis, route)


def tendency(padded, width, spacing, depth):
    middle = lax.slice_in_dim(padded, width, width + depth, axis=-3)
    upper = lax.slice_in_dim(padded, width + 1, width + 1 + depth, axis=-3)
    lower = lax.slice_in_dim(padded, width - 1, width - 1 + depth, axis=-3)
    north = jnp.roll(middle, -1, axis=-2)
    south = jnp.roll(middle, 1, axis=-2)
    east = jnp.roll(middle, -1, axis=-1)
    west = jnp.roll(middle, 1, axis=-1)
    vel_x = lax.slice_in_dim(middle, 0, 1, axis=-4)
    vel_y = lax.slice_in_dim(middle, 1, 2, axis=-4)
    vel_z = lax.slice_in_dim(middle, 2, 3, axis=-4)
    advect = vel_x * (east - west) + vel_y * (north - south) + vel_z * (upper - lower)
    diffuse = upper + lower + north + south + east + west - 6.0 * middle
    return diffuse * (VISCOSITY / (spacing * spacing)) - advect * (0.5 / spacing)


def restrict(field):
    lead = field.shape[:-3]
    depth, rows, cols = field.shape[-3:]
    blocks = field.reshape(lead + (depth // 2, 2, rows // 2, 2, cols // 2, 2))
    return jnp.mean(blocks, axis=(-5, -3, -1))


def prolong(field):
    return jnp.repeat(jnp.repeat(jnp.repeat(field, 2, axis=-3), 2, axis=-2), 2, axis=-1)


def iterate(nodes, first):
    depth = nodes.shape[-3]
    half = depth // 2
    start = nodes[0]
    padded = with_halo(nodes, (("space", 2),), 1)
    f_all = tendency(padded, 1, 1.0, depth)
    v_start = restrict(start)
    coarse_padded = with_halo(v_start, (("space", 1),), 1)
    h_start = tendency(coarse_padded, 1, 2.0, half)
    mid_value = start + STEP * (
        FIRST_ROW[0] * f_all[0] + FIRST_ROW[1] * f_all[1] + FIRST_ROW[2] * f_all[2]
    )
    mid_padded = with_halo(mid_value, (("space", 1),), 1)
    f_mid = tendency(mid_padded, 1, 1.0, depth)
    end_value = mid_value + (
        0.5 * STEP * (f_mid - f_all[1])
        + STEP * (SECOND_ROW[0] * f_all[0] + SECOND_ROW[1] * f_all[1] + SECOND_ROW[2] * f_all[2])
    )
    end_padded = with_halo(end_value, (("space", 1),), 1)
    f_end = tendency(end_padded, 1, 1.0, depth)
    integral = STEP * (f_all[0] / 6.0 + 2.0 / 3.0 * f_mid + f_end / 6.0)
    v_end = restrict(end_value)
    base = restrict(integral) - STEP * h_start
    first_end = v_start + (STEP * h_start + base)

    def advance(count, carry):
        w_start, w_end = carry
        beside_all = with_halo(w_end[None], (("tm", 0), ("space", 2)), 1)[0]
        incoming = lax.slice_in_dim(beside_all, 1, 1 + half, axis=-3)
        next_end = incoming + (STEP * tendency(beside_all, 1, 2.0, half) + base)
        return (jnp.where(first, v_start, incoming), jnp.where(first, first_end, next_end))

    w_start, w_end = lax.fori_loop(0, lax.axis_size("tm") - 1, advance, (v_start, first_end))
    delta_start = w_start - v_start
    delta_end = w_end - v_end
    new_mid = mid_value + prolong(0.5 * (delta_start + delta_end))
    new_end = end_value + prolong(delta_end)
    shifted = passed_along(new_end, "tm", 1)
    new_start = jnp.where(first, start, shifted)
    return jnp.stack([new_start, new_mid, new_end])


def local(u_nodes):
    first = lax.axis_index("tm") == 0
    nodes = u_nodes[0]
    nodes = iterate(nodes, first)
    return nodes[None]


def solution(mesh):
    return jax.shard_map(
        local,
        mesh=mesh,
        in_specs=(P("tm", None, None, "space", None, None),),
        out_specs=P("tm", None, None, "space", None, None),
        check_vma=False,
    )
```

profile of v0, /device:TPU:384, one launch (start us, length us, event | category | flops | bytes accessed | tf_op | source)
XLA Modules:
  0.0 1026.4 jit_solution(16703474687726635209)
XLA Ops:
  13.5 14.5 %collective-permute-start.8 = (f32[3,1,4,64]{3,2,1,0:T(4,128)}, f32[3,1,4,64]{3,2,1,0:T(4,128)}, u32[]{:S(2)}, u32[]{:S(2)}) collective-permute-start(f32[3,1,4,64]{3,2,1,0:T(4,128)} %get-tuple-element.118), channel_id=1, source_target_pairs={{1,0},{2,1},{3,2},{4,3},{5,4},{6,5},{7,6},{8,7},{9,8},{10,9},{11,1... | collective-permute-start | bytes 9224 | tf_op jit(solution)/shard_map/ppermute | solution.py:22
  35.8 14.5 %collective-permute-start.6 = (f32[3,1,8,128]{3,2,1,0:T(8,128)S(1)}, f32[3,1,8,128]{3,2,1,0:T(8,128)S(1)}, u32[]{:S(2)}, u32[]{:S(2)}) collective-permute-start(f32[3,1,8,128]{3,2,1,0:T(8,128)S(1)} %get-tuple-element.105), channel_id=1, source_target_pairs={{1,0},{2,1},{3,2},{4,3},{5,4},{6,5},{7,6},{8,7},{9,8},{10,9},{11,1... | collective-permute-start | bytes 36872 | tf_op jit(solution)/shard_map/ppermute | solution.py:22
  52.2 13.9 %collective-permute-done.7 = f32[3,1,8,128]{3,2,1,0:T(8,128)S(1)} collective-permute-done((f32[3,1,8,128]{3,2,1,0:T(8,128)S(1)}, f32[3,1,8,128]{3,2,1,0:T(8,128)S(1)}, u32[]{:S(2)}, u32[]{:S(2)}) %collective-permute-start.7) | collective-permute-done | bytes 12320 | tf_op jit(solution)/shard_map/ppermute | solution.py:20
  95.1 919.1 %while.12 = (s32[]{:T(128)}, f32[3,2,4,64]{3,2,1,0:T(4,128)}, f32[3,2,4,64]{3,2,1,0:T(4,128)S(1)}, pred[]{:T(512)}, f32[3,2,4,64]{3,2,1,0:T(4,128)S(1)}, /*index...) while((s32[]{:T(128)}, f32[3,2,4,64]{3,2,1,0:T(4,128)}, f32[3,2,4,64]{3,2,1,0:T(4,128)S(1)}, ...), condition=%wide.region_3.4_spmd, body=%wide.region_2.3_spmd.sunk | while | flops 62978 | bytes 387318 | solution.py:94
  114.0 14.0 %collective-permute-done.3 = f32[3,3,1,4,64]{4,3,2,1,0:T(4,128)S(1)} collective-permute-done((f32[3,3,1,4,64]{4,3,2,1,0:T(4,128)S(1)}, f32[3,3,1,4,64]{4,3,2,1,0:T(4,128)S(1)}, u32[]{:S(2)}, u32[]{:S(2)}) %collective-permute-start.3) | collective-permute-done | bytes 9248 | tf_op jit(solution)/shard_map/while/body/eval_jaxpr/ppermute | solution.py:20
  144.0 13.5 %collective-permute-done.3 = f32[3,3,1,4,64]{4,3,2,1,0:T(4,128)S(1)} collective-permute-done((f32[3,3,1,4,64]{4,3,2,1,0:T(4,128)S(1)}, f32[3,3,1,4,64]{4,3,2,1,0:T(4,128)S(1)}, u32[]{:S(2)}, u32[]{:S(2)}) %collective-permute-start.3) | collective-permute-done | bytes 9248 | tf_op jit(solution)/shard_map/while/body/eval_jaxpr/ppermute | solution.py:20
  173.5 13.5 %collective-permute-done.3 = f32[3,3,1,4,64]{4,3,2,1,0:T(4,128)S(1)} collective-permute-done((f32[3,3,1,4,64]{4,3,2,1,0:T(4,128)S(1)}, f32[3,3,1,4,64]{4,3,2,1,0:T(4,128)S(1)}, u32[]{:S(2)}, u32[]{:S(2)}) %collective-permute-start.3) | collective-permute-done | bytes 9248 | tf_op jit(solution)/shard_map/while/body/eval_jaxpr/ppermute | solution.py:20
  203.0 13.5 %collective-permute-done.3 = f32[3,3,1,4,64]{4,3,2,1,0:T(4,128)S(1)} collective-permute-done((f32[3,3,1,4,64]{4,3,2,1,0:T(4,128)S(1)}, f32[3,3,1,4,64]{4,3,2,1,0:T(4,128)S(1)}, u32[]{:S(2)}, u32[]{:S(2)}) %collective-permute-start.3) | collective-permute-done | bytes 9248 | tf_op jit(solution)/shard_map/while/body/eval_jaxpr/ppermute | solution.py:20
  232.5 13.5 %collective-permute-done.3 = f32[3,3,1,4,64]{4,3,2,1,0:T(4,128)S(1)} collective-permute-done((f32[3,3,1,4,64]{4,3,2,1,0:T(4,128)S(1)}, f32[3,3,1,4,64]{4,3,2,1,0:T(4,128)S(1)}, u32[]{:S(2)}, u32[]{:S(2)}) %collective-permute-start.3) | collective-permute-done | bytes 9248 | tf_op jit(solution)/shard_map/while/body/eval_jaxpr/ppermute | solution.py:20
  262.0 13.5 %collective-permute-done.3 = f32[3,3,1,4,64]{4,3,2,1,0:T(4,128)S(1)} collective-permute-done((f32[3,3,1,4,64]{4,3,2,1,0:T(4,128)S(1)}, f32[3,3,1,4,64]{4,3,2,1,0:T(4,128)S(1)}, u32[]{:S(2)}, u32[]{:S(2)}) %collective-permute-start.3) | collective-permute-done | bytes 9248 | tf_op jit(solution)/shard_map/while/body/eval_jaxpr/ppermute | solution.py:20
  291.6 13.5 %collective-permute-done.3 = f32[3,3,1,4,64]{4,3,2,1,0:T(4,128)S(1)} collective-permute-done((f32[3,3,1,4,64]{4,3,2,1,0:T(4,128)S(1)}, f32[3,3,1,4,64]{4,3,2,1,0:T(4,128)S(1)}, u32[]{:S(2)}, u32[]{:S(2)}) %collective-permute-start.3) | collective-permute-done | bytes 9248 | tf_op jit(solution)/shard_map/while/body/eval_jaxpr/ppermute | solution.py:20
  321.1 13.5 %collective-permute-done.3 = f32[3,3,1,4,64]{4,3,2,1,0:T(4,128)S(1)} collective-permute-done((f32[3,3,1,4,64]{4,3,2,1,0:T(4,128)S(1)}, f32[3,3,1,4,64]{4,3,2,1,0:T(4,128)S(1)}, u32[]{:S(2)}, u32[]{:S(2)}) %collective-permute-start.3) | collective-permute-done | bytes 9248 | tf_op jit(solution)/shard_map/while/body/eval_jaxpr/ppermute | solution.py:20
  350.6 13.5 %collective-permute-done.3 = f32[3,3,1,4,64]{4,3,2,1,0:T(4,128)S(1)} collective-permute-done((f32[3,3,1,4,64]{4,3,2,1,0:T(4,128)S(1)}, f32[3,3,1,4,64]{4,3,2,1,0:T(4,128)S(1)}, u32[]{:S(2)}, u32[]{:S(2)}) %collective-permute-start.3) | collective-permute-done | bytes 9248 | tf_op jit(solution)/shard_map/while/body/eval_jaxpr/ppermute | solution.py:20
  380.1 13.5 %collective-permute-done.3 = f32[3,3,1,4,64]{4,3,2,1,0:T(4,128)S(1)} collective-permute-done((f32[3,3,1,4,64]{4,3,2,1,0:T(4,128)S(1)}, f32[3,3,1,4,64]{4,3,2,1,0:T(4,128)S(1)}, u32[]{:S(2)}, u32[]{:S(2)}) %collective-permute-start.3) | collective-permute-done | bytes 9248 | tf_op jit(solution)/shard_map/while/body/eval_jaxpr/ppermute | solution.py:20
  409.6 13.5 %collective-permute-done.3 = f32[3,3,1,4,64]{4,3,2,1,0:T(4,128)S(1)} collective-permute-done((f32[3,3,1,4,64]{4,3,2,1,0:T(4,128)S(1)}, f32[3,3,1,4,64]{4,3,2,1,0:T(4,128)S(1)}, u32[]{:S(2)}, u32[]{:S(2)}) %collective-permute-start.3) | collective-permute-done | bytes 9248 | tf_op jit(solution)/shard_map/while/body/eval_jaxpr/ppermute | solution.py:20
  439.1 13.5 %collective-permute-done.3 = f32[3,3,1,4,64]{4,3,2,1,0:T(4,128)S(1)} collective-permute-done((f32[3,3,1,4,64]{4,3,2,1,0:T(4,128)S(1)}, f32[3,3,1,4,64]{4,3,2,1,0:T(4,128)S(1)}, u32[]{:S(2)}, u32[]{:S(2)}) %collective-permute-start.3) | collective-permute-done | bytes 9248 | tf_op jit(solution)/shard_map/while/body/eval_jaxpr/ppermute | solution.py:20
  468.6 13.5 %collective-permute-done.3 = f32[3,3,1,4,64]{4,3,2,1,0:T(4,128)S(1)} collective-permute-done((f32[3,3,1,4,64]{4,3,2,1,0:T(4,128)S(1)}, f32[3,3,1,4,64]{4,3,2,1,0:T(4,128)S(1)}, u32[]{:S(2)}, u32[]{:S(2)}) %collective-permute-start.3) | collective-permute-done | bytes 9248 | tf_op jit(solution)/shard_map/while/body/eval_jaxpr/ppermute | solution.py:20
  498.1 13.5 %collective-permute-done.3 = f32[3,3,1,4,64]{4,3,2,1,0:T(4,128)S(1)} collective-permute-done((f32[3,3,1,4,64]{4,3,2,1,0:T(4,128)S(1)}, f32[3,3,1,4,64]{4,3,2,1,0:T(4,128)S(1)}, u32[]{:S(2)}, u32[]{:S(2)}) %collective-permute-start.3) | collective-permute-done | bytes 9248 | tf_op jit(solution)/shard_map/while/body/eval_jaxpr/ppermute | solution.py:20
  527.7 13.5 %collective-permute-done.3 = f32[3,3,1,4,64]{4,3,2,1,0:T(4,128)S(1)} collective-permute-done((f32[3,3,1,4,64]{4,3,2,1,0:T(4,128)S(1)}, f32[3,3,1,4,64]{4,3,2,1,0:T(4,128)S(1)}, u32[]{:S(2)}, u32[]{:S(2)}) %collective-permute-start.3) | collective-permute-done | bytes 9248 | tf_op jit(solution)/shard_map/while/body/eval_jaxpr/ppermute | solution.py:20
  557.2 13.5 %collective-permute-done.3 = f32[3,3,1,4,64]{4,3,2,1,0:T(4,128)S(1)} collective-permute-done((f32[3,3,1,4,64]{4,3,2,1,0:T(4,128)S(1)}, f32[3,3,1,4,64]{4,3,2,1,0:T(4,128)S(1)}, u32[]{:S(2)}, u32[]{:S(2)}) %collective-permute-start.3) | collective-permute-done | bytes 9248 | tf_op jit(solution)/shard_map/while/body/eval_jaxpr/ppermute | solution.py:20
  586.7 13.5 %collective-permute-done.3 = f32[3,3,1,4,64]{4,3,2,1,0:T(4,128)S(1)} collective-permute-done((f32[3,3,1,4,64]{4,3,2,1,0:T(4,128)S(1)}, f32[3,3,1,4,64]{4,3,2,1,0:T(4,128)S(1)}, u32[]{:S(2)}, u32[]{:S(2)}) %collective-permute-start.3) | collective-permute-done | bytes 9248 | tf_op jit(solution)/shard_map/while/body/eval_jaxpr/ppermute | solution.py:20
  616.2 13.5 %collective-permute-done.3 = f32[3,3,1,4,64]{4,3,2,1,0:T(4,128)S(1)} collective-permute-done((f32[3,3,1,4,64]{4,3,2,1,0:T(4,128)S(1)}, f32[3,3,1,4,64]{4,3,2,1,0:T(4,128)S(1)}, u32[]{:S(2)}, u32[]{:S(2)}) %collective-permute-start.3) | collective-permute-done | bytes 9248 | tf_op jit(solution)/shard_map/while/body/eval_jaxpr/ppermute | solution.py:20
  645.7 13.5 %collective-permute-done.3 = f32[3,3,1,4,64]{4,3,2,1,0:T(4,128)S(1)} collective-permute-done((f32[3,3,1,4,64]{4,3,2,1,0:T(4,128)S(1)}, f32[3,3,1,4,64]{4,3,2,1,0:T(4,128)S(1)}, u32[]{:S(2)}, u32[]{:S(2)}) %collective-permute-start.3) | collective-permute-done | bytes 9248 | tf_op jit(solution)/shard_map/while/body/eval_jaxpr/ppermute | solution.py:20
  763.8 13.5 %collective-permute-done.3 = f32[3,3,1,4,64]{4,3,2,1,0:T(4,128)S(1)} collective-permute-done((f32[3,3,1,4,64]{4,3,2,1,0:T(4,128)S(1)}, f32[3,3,1,4,64]{4,3,2,1,0:T(4,128)S(1)}, u32[]{:S(2)}, u32[]{:S(2)}) %collective-permute-start.3) | collective-permute-done | bytes 9248 | tf_op jit(solution)/shard_map/while/body/eval_jaxpr/ppermute | solution.py:20
  (587 shorter events, 710.6 us)
Async XLA Ops:
  1.4 32.5 %collective-permute-start.4 = (f32[3,3,1,8,128]{4,3,2,1,0:T(8,128)}, f32[3,3,1,8,128]{4,3,2,1,0:T(8,128)S(1)}, u32[]{:S(2)}, u32[]{:S(2)}) collective-permute-start(f32[3,3,1,8,128]{4,3,2,1,0:T(8,128)} %get-tuple-element.83), channel_id=1, source_target_pairs={{1,0},{2,1},{3,2},{4,3},{5,4},{6,5},{7,6},{8,7},{9,8},{10,9},{11,1... | collective-permute-start | bytes 110600 | tf_op jit(solution)/shard_map/ppermute | solution.py:22
  6.7 27.3 %collective-permute-start.5 = (f32[3,3,1,8,128]{4,3,2,1,0:T(8,128)S(1)}, f32[3,3,1,8,128]{4,3,2,1,0:T(8,128)S(1)}, u32[]{:S(2)}, u32[]{:S(2)}) collective-permute-start(f32[3,3,1,8,128]{4,3,2,1,0:T(8,128)S(1)} %get-tuple-element.82), channel_id=1, source_target_pairs={{0,1},{1,2},{2,3},{3,4},{4,5},{5,6},{6,7},{7,8},{8,9},{9,10},{10,1... | collective-permute-start | bytes 110600 | tf_op jit(solution)/shard_map/ppermute | solution.py:20
  13.5 80.6 %collective-permute-start.8 = (f32[3,1,4,64]{3,2,1,0:T(4,128)}, f32[3,1,4,64]{3,2,1,0:T(4,128)}, u32[]{:S(2)}, u32[]{:S(2)}) collective-permute-start(f32[3,1,4,64]{3,2,1,0:T(4,128)} %get-tuple-element.118), channel_id=1, source_target_pairs={{1,0},{2,1},{3,2},{4,3},{5,4},{6,5},{7,6},{8,7},{9,8},{10,9},{11,1... | collective-permute-start | bytes 9224 | tf_op jit(solution)/shard_map/ppermute | solution.py:22
  28.0 66.2 %collective-permute-start.9 = (f32[3,1,4,64]{3,2,1,0:T(4,128)}, f32[3,1,4,64]{3,2,1,0:T(4,128)}, u32[]{:S(2)}, u32[]{:S(2)}) collective-permute-start(f32[3,1,4,64]{3,2,1,0:T(4,128)} %get-tuple-element.119), channel_id=1, source_target_pairs={{0,1},{1,2},{2,3},{3,4},{4,5},{5,6},{6,7},{7,8},{8,9},{9,10},{10,1... | collective-permute-start | bytes 9224 | tf_op jit(solution)/shard_map/ppermute | solution.py:20
  35.8 16.4 %collective-permute-start.6 = (f32[3,1,8,128]{3,2,1,0:T(8,128)S(1)}, f32[3,1,8,128]{3,2,1,0:T(8,128)S(1)}, u32[]{:S(2)}, u32[]{:S(2)}) collective-permute-start(f32[3,1,8,128]{3,2,1,0:T(8,128)S(1)} %get-tuple-element.105), channel_id=1, source_target_pairs={{1,0},{2,1},{3,2},{4,3},{5,4},{6,5},{7,6},{8,7},{9,8},{10,9},{11,1... | collective-permute-start | bytes 36872 | tf_op jit(solution)/shard_map/ppermute | solution.py:22
  72.0 16.2 %collective-permute-start.11 = (f32[3,1,8,128]{3,2,1,0:T(8,128)}, f32[3,1,8,128]{3,2,1,0:T(8,128)}, u32[]{:S(2)}, u32[]{:S(2)}) collective-permute-start(f32[3,1,8,128]{3,2,1,0:T(8,128)} %get-tuple-element.95), channel_id=1, source_target_pairs={{0,1},{1,2},{2,3},{3,4},{4,5},{5,6},{6,7},{7,8},{8,9},{9,10},{10,1... | collective-permute-start | bytes 36872 | tf_op jit(solution)/shard_map/ppermute | solution.py:20
  112.0 15.9 %collective-permute-start.3 = (f32[3,3,1,4,64]{4,3,2,1,0:T(4,128)S(1)}, f32[3,3,1,4,64]{4,3,2,1,0:T(4,128)S(1)}, u32[]{:S(2)}, u32[]{:S(2)}) collective-permute-start(f32[3,3,1,4,64]{4,3,2,1,0:T(4,128)S(1)} %get-tuple-element.188), channel_id=1, source_target_pairs={{0,1},{1,2},{2,3},{3,4},{4,5},{5,6},{6,7},{7,8},{8,9},{9,10},{10,1... | collective-permute-start | bytes 27656 | tf_op jit(solution)/shard_map/while/body/eval_jaxpr/ppermute | solution.py:20
  141.6 15.9 %collective-permute-start.3 = (f32[3,3,1,4,64]{4,3,2,1,0:T(4,128)S(1)}, f32[3,3,1,4,64]{4,3,2,1,0:T(4,128)S(1)}, u32[]{:S(2)}, u32[]{:S(2)}) collective-permute-start(f32[3,3,1,4,64]{4,3,2,1,0:T(4,128)S(1)} %get-tuple-element.188), channel_id=1, source_target_pairs={{0,1},{1,2},{2,3},{3,4},{4,5},{5,6},{6,7},{7,8},{8,9},{9,10},{10,1... | collective-permute-start | bytes 27656 | tf_op jit(solution)/shard_map/while/body/eval_jaxpr/ppermute | solution.py:20
  171.1 15.9 %collective-permute-start.3 = (f32[3,3,1,4,64]{4,3,2,1,0:T(4,128)S(1)}, f32[3,3,1,4,64]{4,3,2,1,0:T(4,128)S(1)}, u32[]{:S(2)}, u32[]{:S(2)}) collective-permute-start(f32[3,3,1,4,64]{4,3,2,1,0:T(4,128)S(1)} %get-tuple-element.188), channel_id=1, source_target_pairs={{0,1},{1,2},{2,3},{3,4},{4,5},{5,6},{6,7},{7,8},{8,9},{9,10},{10,1... | collective-permute-start | bytes 27656 | tf_op jit(solution)/shard_map/while/body/eval_jaxpr/ppermute | solution.py:20
  200.6 15.9 %collective-permute-start.3 = (f32[3,3,1,4,64]{4,3,2,1,0:T(4,128)S(1)}, f32[3,3,1,4,64]{4,3,2,1,0:T(4,128)S(1)}, u32[]{:S(2)}, u32[]{:S(2)}) collective-permute-start(f32[3,3,1,4,64]{4,3,2,1,0:T(4,128)S(1)} %get-tuple-element.188), channel_id=1, source_target_pairs={{0,1},{1,2},{2,3},{3,4},{4,5},{5,6},{6,7},{7,8},{8,9},{9,10},{10,1... | collective-permute-start | bytes 27656 | tf_op jit(solution)/shard_map/while/body/eval_jaxpr/ppermute | solution.py:20
  230.1 15.9 %collective-permute-start.3 = (f32[3,3,1,4,64]{4,3,2,1,0:T(4,128)S(1)}, f32[3,3,1,4,64]{4,3,2,1,0:T(4,128)S(1)}, u32[]{:S(2)}, u32[]{:S(2)}) collective-permute-start(f32[3,3,1,4,64]{4,3,2,1,0:T(4,128)S(1)} %get-tuple-element.188), channel_id=1, source_target_pairs={{0,1},{1,2},{2,3},{3,4},{4,5},{5,6},{6,7},{7,8},{8,9},{9,10},{10,1... | collective-permute-start | bytes 27656 | tf_op jit(solution)/shard_map/while/body/eval_jaxpr/ppermute | solution.py:20
  289.1 15.9 %collective-permute-start.3 = (f32[3,3,1,4,64]{4,3,2,1,0:T(4,128)S(1)}, f32[3,3,1,4,64]{4,3,2,1,0:T(4,128)S(1)}, u32[]{:S(2)}, u32[]{:S(2)}) collective-permute-start(f32[3,3,1,4,64]{4,3,2,1,0:T(4,128)S(1)} %get-tuple-element.188), channel_id=1, source_target_pairs={{0,1},{1,2},{2,3},{3,4},{4,5},{5,6},{6,7},{7,8},{8,9},{9,10},{10,1... | collective-permute-start | bytes 27656 | tf_op jit(solution)/shard_map/while/body/eval_jaxpr/ppermute | solution.py:20
  318.6 15.9 %collective-permute-start.3 = (f32[3,3,1,4,64]{4,3,2,1,0:T(4,128)S(1)}, f32[3,3,1,4,64]{4,3,2,1,0:T(4,128)S(1)}, u32[]{:S(2)}, u32[]{:S(2)}) collective-permute-start(f32[3,3,1,4,64]{4,3,2,1,0:T(4,128)S(1)} %get-tuple-element.188), channel_id=1, source_target_pairs={{0,1},{1,2},{2,3},{3,4},{4,5},{5,6},{6,7},{7,8},{8,9},{9,10},{10,1... | collective-permute-start | bytes 27656 | tf_op jit(solution)/shard_map/while/body/eval_jaxpr/ppermute | solution.py:20
  348.2 15.9 %collective-permute-start.3 = (f32[3,3,1,4,64]{4,3,2,1,0:T(4,128)S(1)}, f32[3,3,1,4,64]{4,3,2,1,0:T(4,128)S(1)}, u32[]{:S(2)}, u32[]{:S(2)}) collective-permute-start(f32[3,3,1,4,64]{4,3,2,1,0:T(4,128)S(1)} %get-tuple-element.188), channel_id=1, source_target_pairs={{0,1},{1,2},{2,3},{3,4},{4,5},{5,6},{6,7},{7,8},{8,9},{9,10},{10,1... | collective-permute-start | bytes 27656 | tf_op jit(solution)/shard_map/while/body/eval_jaxpr/ppermute | solution.py:20
  377.7 15.9 %collective-permute-start.3 = (f32[3,3,1,4,64]{4,3,2,1,0:T(4,128)S(1)}, f32[3,3,1,4,64]{4,3,2,1,0:T(4,128)S(1)}, u32[]{:S(2)}, u32[]{:S(2)}) collective-permute-start(f32[3,3,1,4,64]{4,3,2,1,0:T(4,128)S(1)} %get-tuple-element.188), channel_id=1, source_target_pairs={{0,1},{1,2},{2,3},{3,4},{4,5},{5,6},{6,7},{7,8},{8,9},{9,10},{10,1... | collective-permute-start | bytes 27656 | tf_op jit(solution)/shard_map/while/body/eval_jaxpr/ppermute | solution.py:20
  407.2 15.9 %collective-permute-start.3 = (f32[3,3,1,4,64]{4,3,2,1,0:T(4,128)S(1)}, f32[3,3,1,4,64]{4,3,2,1,0:T(4,128)S(1)}, u32[]{:S(2)}, u32[]{:S(2)}) collective-permute-start(f32[3,3,1,4,64]{4,3,2,1,0:T(4,128)S(1)} %get-tuple-element.188), channel_id=1, source_target_pairs={{0,1},{1,2},{2,3},{3,4},{4,5},{5,6},{6,7},{7,8},{8,9},{9,10},{10,1... | collective-permute-start | bytes 27656 | tf_op jit(solution)/shard_map/while/body/eval_jaxpr/ppermute | solution.py:20
  436.7 15.9 %collective-permute-start.3 = (f32[3,3,1,4,64]{4,3,2,1,0:T(4,128)S(1)}, f32[3,3,1,4,64]{4,3,2,1,0:T(4,128)S(1)}, u32[]{:S(2)}, u32[]{:S(2)}) collective-permute-start(f32[3,3,1,4,64]{4,3,2,1,0:T(4,128)S(1)} %get-tuple-element.188), channel_id=1, source_target_pairs={{0,1},{1,2},{2,3},{3,4},{4,5},{5,6},{6,7},{7,8},{8,9},{9,10},{10,1... | collective-permute-start | bytes 27656 | tf_op jit(solution)/shard_map/while/body/eval_jaxpr/ppermute | solution.py:20
  466.2 15.9 %collective-permute-start.3 = (f32[3,3,1,4,64]{4,3,2,1,0:T(4,128)S(1)}, f32[3,3,1,4,64]{4,3,2,1,0:T(4,128)S(1)}, u32[]{:S(2)}, u32[]{:S(2)}) collective-permute-start(f32[3,3,1,4,64]{4,3,2,1,0:T(4,128)S(1)} %get-tuple-element.188), channel_id=1, source_target_pairs={{0,1},{1,2},{2,3},{3,4},{4,5},{5,6},{6,7},{7,8},{8,9},{9,10},{10,1... | collective-permute-start | bytes 27656 | tf_op jit(solution)/shard_map/while/body/eval_jaxpr/ppermute | solution.py:20
  495.7 15.9 %collective-permute-start.3 = (f32[3,3,1,4,64]{4,3,2,1,0:T(4,128)S(1)}, f32[3,3,1,4,64]{4,3,2,1,0:T(4,128)S(1)}, u32[]{:S(2)}, u32[]{:S(2)}) collective-permute-start(f32[3,3,1,4,64]{4,3,2,1,0:T(4,128)S(1)} %get-tuple-element.188), channel_id=1, source_target_pairs={{0,1},{1,2},{2,3},{3,4},{4,5},{5,6},{6,7},{7,8},{8,9},{9,10},{10,1... | collective-permute-start | bytes 27656 | tf_op jit(solution)/shard_map/while/body/eval_jaxpr/ppermute | solution.py:20
  525.2 15.9 %collective-permute-start.3 = (f32[3,3,1,4,64]{4,3,2,1,0:T(4,128)S(1)}, f32[3,3,1,4,64]{4,3,2,1,0:T(4,128)S(1)}, u32[]{:S(2)}, u32[]{:S(2)}) collective-permute-start(f32[3,3,1,4,64]{4,3,2,1,0:T(4,128)S(1)} %get-tuple-element.188), channel_id=1, source_target_pairs={{0,1},{1,2},{2,3},{3,4},{4,5},{5,6},{6,7},{7,8},{8,9},{9,10},{10,1... | collective-permute-start | bytes 27656 | tf_op jit(solution)/shard_map/while/body/eval_jaxpr/ppermute | solution.py:20
  584.3 15.9 %collective-permute-start.3 = (f32[3,3,1,4,64]{4,3,2,1,0:T(4,128)S(1)}, f32[3,3,1,4,64]{4,3,2,1,0:T(4,128)S(1)}, u32[]{:S(2)}, u32[]{:S(2)}) collective-permute-start(f32[3,3,1,4,64]{4,3,2,1,0:T(4,128)S(1)} %get-tuple-element.188), channel_id=1, source_target_pairs={{0,1},{1,2},{2,3},{3,4},{4,5},{5,6},{6,7},{7,8},{8,9},{9,10},{10,1... | collective-permute-start | bytes 27656 | tf_op jit(solution)/shard_map/while/body/eval_jaxpr/ppermute | solution.py:20
  613.8 15.9 %collective-permute-start.3 = (f32[3,3,1,4,64]{4,3,2,1,0:T(4,128)S(1)}, f32[3,3,1,4,64]{4,3,2,1,0:T(4,128)S(1)}, u32[]{:S(2)}, u32[]{:S(2)}) collective-permute-start(f32[3,3,1,4,64]{4,3,2,1,0:T(4,128)S(1)} %get-tuple-element.188), channel_id=1, source_target_pairs={{0,1},{1,2},{2,3},{3,4},{4,5},{5,6},{6,7},{7,8},{8,9},{9,10},{10,1... | collective-permute-start | bytes 27656 | tf_op jit(solution)/shard_map/while/body/eval_jaxpr/ppermute | solution.py:20
  643.3 15.9 %collective-permute-start.3 = (f32[3,3,1,4,64]{4,3,2,1,0:T(4,128)S(1)}, f32[3,3,1,4,64]{4,3,2,1,0:T(4,128)S(1)}, u32[]{:S(2)}, u32[]{:S(2)}) collective-permute-start(f32[3,3,1,4,64]{4,3,2,1,0:T(4,128)S(1)} %get-tuple-element.188), channel_id=1, source_target_pairs={{0,1},{1,2},{2,3},{3,4},{4,5},{5,6},{6,7},{7,8},{8,9},{9,10},{10,1... | collective-permute-start | bytes 27656 | tf_op jit(solution)/shard_map/while/body/eval_jaxpr/ppermute | solution.py:20
  761.3 15.9 %collective-permute-start.3 = (f32[3,3,1,4,64]{4,3,2,1,0:T(4,128)S(1)}, f32[3,3,1,4,64]{4,3,2,1,0:T(4,128)S(1)}, u32[]{:S(2)}, u32[]{:S(2)}) collective-permute-start(f32[3,3,1,4,64]{4,3,2,1,0:T(4,128)S(1)} %get-tuple-element.188), channel_id=1, source_target_pairs={{0,1},{1,2},{2,3},{3,4},{4,5},{5,6},{6,7},{7,8},{8,9},{9,10},{10,1... | collective-permute-start | bytes 27656 | tf_op jit(solution)/shard_map/while/body/eval_jaxpr/ppermute | solution.py:20
  (114 other events, 1780.8 us)
where the time goes:
time: 1030 us
  waiting for transfers between devices  605 us (59%)
  starting transfers between devices  363 us (35%)
  local copies, waits for them, and re-layouts  28.4 us (3%)
  other arithmetic  27.5 us (3%)
    ppermute x66, waiting for transfers between devices, with_halo(): lax.ppermute(tail, axis, [(i, (i + 1) % count) for i in range(ends)])  597 us
    ppermute x66, starting transfers between devices, with_halo(): lax.ppermute(tail, axis, [(i, (i + 1) % count) for i in range(ends)])  202 us
    ppermute x66, starting transfers between devices, with_halo(): lax.ppermute(head, axis, [((i + 1) % count, i) for i in range(ends)])  159 us
  transfers between devices with their start and end apart: 133, of which 65 were waited for; matrix products, arithmetic and copies ran while one was open for 2% of the time, Pallas kernels for 0%

commit v1 on v0

v1 whole, which is shorter than its diff:
```python
import functools
import operator

import jax
import jax.numpy as jnp
from jax import lax
from jax.experimental import pallas as pl
from jax.experimental.pallas import tpu as pltpu
from jax.sharding import PartitionSpec as P

STEP = 0.2
VISCOSITY = 0.1
FIRST_ROW = (5.0 / 24.0, 1.0 / 3.0, -1.0 / 24.0)
SECOND_ROW = (-1.0 / 24.0, 1.0 / 3.0, 5.0 / 24.0)

GRAY = (0, 1, 3, 2)
WIDE = 3
PARAMS = pltpu.CompilerParams(vmem_limit_bytes=24 * 1024 * 1024)
GROUPS = 4
CORNERS = (8, 12, 16, 24)


def at_x(tile, shift):
    return pltpu.roll(tile, (-shift) % 128, 1)


def at_y(tile, shift):
    return pltpu.roll(tile, (-shift) % 8, 0)


def parities():
    row = lax.broadcasted_iota(jnp.int32, (8, 128), 0) & 1
    col = lax.broadcasted_iota(jnp.int32, (8, 128), 1) & 1
    return row, col


def swap_x(tile, odd_x):
    return jnp.where(odd_x, at_x(tile, -1), at_x(tile, 1))


def swap_y(tile, odd_y):
    return jnp.where(odd_y, at_y(tile, -1), at_y(tile, 1))


def rates(vel, upper, middle, lower, spacing, stride):
    north, south = at_y(middle, stride), at_y(middle, -stride)
    east, west = at_x(middle, stride), at_x(middle, -stride)
    advect = vel[0] * (east - west) + vel[1] * (north - south) + vel[2] * (upper - lower)
    diffuse = (upper + lower) + (north + south) + (east + west) - 6.0 * middle
    return diffuse * (VISCOSITY / (spacing * spacing)) - advect * (0.5 / spacing)


def tendency(planes, low, high, spacing, stride):
    out = [{} for _ in range(3)]
    for z in range(low, high):
        vel = [planes[c][z] for c in range(3)]
        for c in range(3):
            out[c][z] = rates(vel, planes[c][z + 1], planes[c][z], planes[c][z - 1], spacing, stride)
    return out


def restrict_pair(first, second, odd_y, odd_x):
    total = first + second
    total = total + swap_y(total, odd_y)
    total = total + swap_x(total, odd_x)
    return total * 0.125


def fine_kernel(near_ref, side_ref, nodes_ref, mid_ref, end_ref, start_c_ref, end_c_ref, packed_ref):
    here = lax.axis_index("space")
    last = lax.axis_size("space") - 1
    even = here % 2 == 0
    is_first = lax.axis_index("tm") == 0
    row, col = parities()
    odd_y, odd_x = row == 1, col == 1
    keep_low = here > 0
    keep_high = here < last
    def load(node):
        planes = [{} for _ in range(3)]
        for c in range(3):
            for z in range(-3, 7):
                if z < 0:
                    at = node, c, z + WIDE
                    planes[c][z] = jnp.where(even, side_ref[at], near_ref[at])
                elif z < 4:
                    planes[c][z] = nodes_ref[node, c, z]
                else:
                    at = node, c, z - 4
                    planes[c][z] = jnp.where(even, near_ref[at], side_ref[at])
        return planes

    def inside(tile, z):
        if z < 0:
            return jnp.where(keep_low, tile, 0.0)
        if z > 3:
            return jnp.where(keep_high, tile, 0.0)
        return tile

    start = load(0)
    f0 = tendency(start, -2, 6, 1.0, 1)
    f1 = tendency(load(1), -2, 6, 1.0, 1)
    f2 = tendency(load(2), -2, 6, 1.0, 1)
    mid = [{} for _ in range(3)]
    for c in range(3):
        for z in range(-2, 6):
            value = start[c][z] + STEP * (
                FIRST_ROW[0] * f0[c][z] + FIRST_ROW[1] * f1[c][z] + FIRST_ROW[2] * f2[c][z]
            )
            mid[c][z] = inside(value, z)
    f_mid = tendency(mid, -1, 5, 1.0, 1)
    end = [{} for _ in range(3)]
    for c in range(3):
        for z in range(-1, 5):
            value = mid[c][z] + (
                0.5 * STEP * (f_mid[c][z] - f1[c][z])
                + STEP * (SECOND_ROW[0] * f0[c][z] + SECOND_ROW[1] * f1[c][z] + SECOND_ROW[2] * f2[c][z])
            )
            end[c][z] = inside(value, z)
    f_end = tendency(end, 0, 4, 1.0, 1)
    coarse = [
        {k: restrict_pair(start[c][2 * k], start[c][2 * k + 1], odd_y, odd_x) for k in range(-1, 3)} for c in range(3)
    ]
    h_start = tendency(coarse, 0, 2, 2.0, 2)
    planes = []
    for c in range(3):
        for z in range(4):
            mid_ref[c, z] = mid[c][z]
            end_ref[c, z] = end[c][z]
        for k in range(2):
            start_c_ref[c, k] = coarse[c][k]
            end_c_ref[c, k] = restrict_pair(end[c][2 * k], end[c][2 * k + 1], odd_y, odd_x)
            integral = [
                STEP * (f0[c][z] / 6.0 + (2.0 / 3.0) * f_mid[c][z] + f_end[c][z] / 6.0) for z in (2 * k, 2 * k + 1)
            ]
            base = restrict_pair(integral[0], integral[1], odd_y, odd_x) - STEP * h_start[c][k]
            first_end = coarse[c][k] + (STEP * h_start[c][k] + base)
            planes.append(jnp.where(is_first, first_end, base))
    group = here // 4
    own = group ^ (group >> 1)
    place = (row * 2 + col) ^ own
    packed_ref[0] = jnp.where(
        place == 0, planes[0], jnp.where(place == 1, planes[1], jnp.where(place == 2, planes[2], planes[3]))
    )
    packed_ref[1] = jnp.where(place == 0, planes[4], jnp.where(place == 1, planes[5], 0.0))


def merge_kernel(own_ref, other_ref, column_ref):
    column_ref[0] = own_ref[0]
    column_ref[1] = other_ref[0]
    column_ref[2] = own_ref[1] + other_ref[1]


def spread_kernel(column_ref, passed_ref, copies_ref):
    tiles = column_ref[0], column_ref[1] + passed_ref[0], column_ref[2] + passed_ref[1]
    for i in range(copies_ref.shape[0]):
        for n in range(3):
            copies_ref[i, n] = tiles[n]


def unpacker(own_ref, other_ref, odd_y, odd_x, slot, core=None):
    here = lax.axis_index("space")
    half_z = here // 8

    def moved(tile, by):
        if by & 1:
            tile = swap_x(tile, odd_x)
        if by & 2:
            tile = swap_y(tile, odd_y)
        return tile

    def unpack(i):
        tiles = [[None] * 8 for _ in range(3)]
        for j in range(4):
            for half in range(2):
                sent = []
                for g in range(4):
                    slab = 4 * g + j
                    at = i * 4 + (slab % 8) // 2, 2 if half else (slab // 8) ^ half_z
                    if core is None:
                        sent.append(jnp.where(here % 2 == slab % 2, own_ref[at], other_ref[at]))
                    else:
                        sent.append(own_ref[at] if core == slab % 2 else other_ref[at])
                for q in range(4 if half == 0 else 2):
                    place = slot ^ q
                    merged = jnp.where(
                        place == GRAY[0],
                        sent[0],
                        jnp.where(place == GRAY[1], sent[1], jnp.where(place == GRAY[2], sent[2], sent[3])),
                    )
                    plane = 4 * half + q
                    tiles[plane // 2][2 * j + plane % 2] = moved(merged, q)
        return tiles

    return unpack


def chain_step(flat, base, slot):
    now = [list(flat[8 * c : 8 * c + 8]) for c in range(3)]
    planes = [{k: now[c][k] for k in range(8)} for c in range(3)]
    for c in range(3):
        top = now[c][0]
        planes[c][8] = jnp.where(
            slot == GRAY[0],
            at_x(top, 1),
            jnp.where(slot == GRAY[1], at_y(top, 1), jnp.where(slot == GRAY[2], at_x(top, -1), 0.0)),
        )
        low = now[c][7]
        planes[c][-1] = jnp.where(
            slot == GRAY[1],
            at_x(low, -1),
            jnp.where(slot == GRAY[2], at_y(low, -1), jnp.where(slot == GRAY[3], at_x(low, 1), 0.0)),
        )
    spread = STEP * VISCOSITY / 4.0
    after = []
    vel = [[(STEP * 0.25) * planes[c][k] for k in range(8)] for c in range(3)]
    for c in range(3):
        for k in range(8):
            middle, upper, lower = planes[c][k], planes[c][k + 1], planes[c][k - 1]
            north, south = at_y(middle, 2), at_y(middle, -2)
            east, west = at_x(middle, 2), at_x(middle, -2)
            around = (upper + lower) + (north + south) + (east + west)
            advect = vel[0][k] * (east - west) + vel[1][k] * (north - south) + vel[2][k] * (upper - lower)
            after.append((base[c][k] + (1.0 - 6.0 * spread) * middle) + (spread * around - advect))
    return tuple(after)


def flat_tiles(tiles):
    return tuple(tile for row in tiles for tile in row)


def unpack_kernel(count, own_ref, other_ref, base_ref):
    row, col = parities()
    unpack = unpacker(own_ref, other_ref, row == 1, col == 1, row * 2 + col)
    for i in range(count):
        for n, tile in enumerate(flat_tiles(unpack(i))):
            base_ref[i, n] = tile


def stored(base_ref, i):
    return [[base_ref[i, 8 * c + k] for k in range(8)] for c in range(3)]


def runs_wave(wave, count):
    return (lax.axis_index("tm") // count == wave) & (lax.axis_index("space") % 2 == 0)


def first_wave_kernel(count, own_ref, other_ref, out_ref):
    row, col = parities()
    slot = row * 2 + col
    unpack = unpacker(own_ref, other_ref, row == 1, col == 1, slot, 0)

    @pl.when(runs_wave(0, count))
    def _():
        state = flat_tiles(unpack(0))
        for i in range(1, count):
            state = chain_step(state, unpack(i), slot)
        for n in range(24):
            out_ref[n] = state[n]


def wave_kernel(wave, count, base_ref, state_ref, out_ref):
    row, col = parities()
    slot = row * 2 + col

    @pl.when(runs_wave(wave, count))
    def _():
        state = tuple(state_ref[n] for n in range(24))
        for i in range(count):
            state = chain_step(state, stored(base_ref, i), slot)
        for n in range(24):
            out_ref[n] = state[n]


def last_kernel(
    count, base_ref, state_ref, given_ref, late_ref, nodes_ref, mid_ref, end_ref, prev_ref, edge_ref,
    start_c_ref, end_c_ref, out_ref, states,
):
    here = lax.axis_index("space")
    slice_id = lax.axis_index("tm")
    row, col = parities()
    odd_y, odd_x = row == 1, col == 1
    slot = row * 2 + col
    own = slice_id % count
    in_first = slice_id // count == 0
    is_last = slice_id // count == GROUPS - 1
    at_corner = functools.reduce(operator.or_, [slice_id == i for i in CORNERS])

    def keep(i, flat):
        for n in range(24):
            states[i, n] = flat[n]

    from_own = here % 2 == 0
    state = tuple(
        jnp.where(from_own, state_ref[n], jnp.where(is_last, late_ref[n], given_ref[n])) for n in range(24)
    )
    keep(0, state)
    for i in range(count):
        base = stored(base_ref, i)
        state = chain_step(state, base, slot)
        if i == 0:
            state = tuple(jnp.where(in_first, b, after) for b, after in zip(flat_tiles(base), state))
        keep(i + 1, state)

    group = here // 4
    code = group ^ (group >> 1)
    own_y, own_x = code >> 1, code & 1
    base_k = 2 * (here % 4)

    def spread(tile):
        tile = jnp.where(row == own_y, tile, swap_y(tile, odd_y))
        return jnp.where(col == own_x, tile, swap_x(tile, odd_x))

    is_first = slice_id == 0
    for c in range(3):
        for k in range(2):
            w_end = spread(states[own + 1, 8 * c + base_k + k])
            v_start = start_c_ref[c, k]
            w_start = jnp.where(is_first, v_start, spread(states[own, 8 * c + base_k + k]))
            delta_start = w_start - v_start
            delta_end = w_end - end_c_ref[c, k]
            half = 0.5 * (delta_start + delta_end)
            handed = [jnp.where(at_corner, edge_ref[c, 2 * k + i], prev_ref[c, 2 * k + i]) for i in range(2)]
            delta_prev = w_start - restrict_pair(handed[0], handed[1], odd_y, odd_x)
            for i in range(2):
                z = 2 * k + i
                out_ref[0, 0, c, z] = jnp.where(is_first, nodes_ref[0, c, z], handed[i] + delta_prev)
                out_ref[0, 1, c, z] = mid_ref[c, z] + half
                out_ref[0, 2, c, z] = end_ref[c, z] + delta_end


def vmem(count):
    return [pl.BlockSpec(memory_space=pltpu.VMEM)] * count


def local(u_nodes):
    nodes = u_nodes[0]
    depth = nodes.shape[2]
    slabs = lax.axis_size("space")
    slices = lax.axis_size("tm")
    tile = nodes.shape[3:]
    shape = lambda *lead: jax.ShapeDtypeStruct(lead + tile, jnp.float32)
    both = ("tm", "space")
    middle = slabs // 2
    even = lax.axis_index("space") % 2 == 0
    top, bottom = nodes[:, :, depth - WIDE :], nodes[:, :, :WIDE]

    def swaps(pairs):
        return [(i, j) for i, j in pairs] + [(j, i) for i, j in pairs]

    to_side = jnp.where(even, bottom, top)
    side = lax.ppermute(to_side, "space", swaps([(i, i + 1) for i in range(1, slabs - 1, 2)]))
    near = lax.ppermute(jnp.where(even, top, bottom), "space", swaps([(i, i + 1) for i in range(0, slabs, 2)]))
    mid, end, start_c, end_c, packed = pl.pallas_call(
        fine_kernel,
        out_shape=[shape(3, 4), shape(3, 4), shape(3, 2), shape(3, 2), shape(2)],
        in_specs=vmem(3),
        out_specs=vmem(5),
        compiler_params=PARAMS,
        name="fine",
    )(near, side, nodes)
    across = lax.ppermute(packed, "space", [(i, (i + middle) % slabs) for i in range(1, slabs)])
    beside = lax.ppermute(packed, "space", [(0, middle + 1)])
    column = pl.pallas_call(
        merge_kernel, out_shape=shape(3), in_specs=vmem(2), out_specs=vmem(1)[0], compiler_params=PARAMS, name="merge"
    )(packed, across)
    column, beside = lax.optimization_barrier((column, beside))
    passed = lax.ppermute(beside, "space", [(middle + 1, middle)])
    copies = pl.pallas_call(
        spread_kernel,
        out_shape=shape(32, 3),
        in_specs=vmem(2),
        out_specs=vmem(1)[0],
        compiler_params=PARAMS,
        name="spread",
    )(column, passed)

    device = lambda zl, y, zh, x, core: (zl * 4 + y) * slabs + zh * 8 + x * 2 + core
    layers = [
        [device(2 * g + zl, y, zh, x, core) for zl in range(2) for y in range(4) for x in range(4)]
        for g in range(GROUPS)
        for zh in range(2)
        for core in range(2)
    ]
    own = lax.all_to_all(copies, both, 0, 0, axis_index_groups=layers)
    edge = lax.ppermute(end, "tm", [(i - 1, i) for i in CORNERS])
    own, edge = lax.optimization_barrier((own, edge))
    other = lax.ppermute(own, "space", swaps([(i, i + 1) for i in range(0, slabs, 2)]))
    count = slices // GROUPS

    def cores(groups):
        return [((g * count + i) * slabs + s) for g in groups for i in range(count) for s in range(0, slabs, 2)]

    after = pl.pallas_call(
        functools.partial(first_wave_kernel, count),
        out_shape=shape(24),
        in_specs=vmem(2),
        out_specs=vmem(1)[0],
        compiler_params=PARAMS,
        name="wave",
    )(own, other)
    own, after = lax.optimization_barrier((own, after))
    bases = pl.pallas_call(
        functools.partial(unpack_kernel, count),
        out_shape=shape(count, 24),
        in_specs=vmem(2),
        out_specs=vmem(1)[0],
        compiler_params=PARAMS,
        cost_estimate=pl.CostEstimate(flops=10_000_000, bytes_accessed=10_000_000, transcendentals=0),
        name="unpack",
    )(own, other)
    state = lax.ppermute(after, both, [(i, i + count * slabs) for i in cores([0])])
    for wave in range(1, GROUPS - 1):
        after = pl.pallas_call(
            functools.partial(wave_kernel, wave, count),
            out_shape=shape(24),
            in_specs=vmem(2),
            out_specs=vmem(1)[0],
            compiler_params=PARAMS,
            name="wave",
        )(bases, state)
        early, after = lax.optimization_barrier((state, after))
        if wave == 1:
            handed, after = lax.optimization_barrier((end, after))
            prev = lax.ppermute(handed, "tm", [(i, i + 1) for i in range(slices - 1) if i + 1 not in CORNERS])
        moved = lax.ppermute(after, both, [(i, i + count * slabs) for i in cores([wave])])
        if wave == 1:
            prev, moved = lax.optimization_barrier((prev, moved))
        state = moved + early
    late = lax.ppermute(after, both, [(i, i + count * slabs + 1) for i in cores([GROUPS - 2])])
    given = lax.ppermute(early, both, [(i, i + 1) for i in cores(range(1, GROUPS - 1))])
    return pl.pallas_call(
        functools.partial(last_kernel, count),
        out_shape=shape(1, 3, 3, 4),
        in_specs=vmem(11),
        out_specs=vmem(1)[0],
        scratch_shapes=[pltpu.VMEM((count + 1, 24) + tile, jnp.float32)],
        compiler_params=PARAMS,
        name="last",
    )(bases, state, given, late, nodes, mid, end, prev, edge, start_c, end_c)


def solution(mesh):
    return jax.shard_map(
        local,
        mesh=mesh,
        in_specs=(P("tm", None, None, "space", None, None),),
        out_specs=P("tm", None, None, "space", None, None),
        check_vma=False,
    )
```

time: 1030 us -> 77 us (0.07)
  the two profiles are of different devices: /device:TPU:384 before, /device:TPU:225 now
where the time goes in v1:
time: 77 us; the launch traced here: 76.5 us
  starting transfers between devices  45.7 us (59%)
  waiting for transfers between devices  26.3 us (34%)
  Pallas kernels  3.22 us (4%)
  other arithmetic  1.09 us (1%)
    all_to_all x1, starting transfers between devices, local(): own = lax.all_to_all(copies, both, 0, 0, axis_index_groups=layers)  17.6 us
    ppermute x1, starting transfers between devices, local(): lax.ppermute(packed, 'space', [(i, (i + middle) % slabs) for i in range(1...  12.5 us
    ppermute x1, waiting for transfers between devices, local(): lax.ppermute(after, both, [(i, i + count * slabs + 1) for i in cores([GRO...  11.1 us
    all_to_all x1, waiting for transfers between devices, local(): own = lax.all_to_all(copies, both, 0, 0, axis_index_groups=layers)  7.08 us
    ppermute x1, waiting for transfers between devices, local(): lax.ppermute(handed, 'tm', [(i, i + 1) for i in range(slices - 1) if i +...  4.82 us
    ppermute x1, starting transfers between devices, local(): lax.ppermute(to_side, 'space', swaps([(i, i + 1) for i in range(1, slabs...  3.68 us
    ppermute x1, starting transfers between devices, local(): lax.ppermute(handed, 'tm', [(i, i + 1) for i in range(slices - 1) if i +...  2.12 us
    ppermute x1, starting transfers between devices, local(): lax.ppermute(jnp.where(even, top, bottom), 'space', swaps([(i, i + 1) for...  1.92 us
  transfers between devices with their start and end apart: 14, of which 7 were waited for; matrix products, arithmetic and copies ran while one was open for 0% of the time, Pallas kernels for 0%

profile of v1, /device:TPU:225, one launch (start us, length us, event | category | flops | bytes accessed | tf_op | source)
XLA Modules:
  0.0 76.5 jit_solution(2444221383102789235)
XLA Ops:
  0.0 1.1 %slice_select_fusion = (f32[3,3,3,8,128]{4,3,2,1,0:T(8,128)S(1)}, f32[3,3,3,8,128]{4,3,2,1,0:T(8,128)S(1)}) fusion(f32[3,3,4,8,128]{4,3,2,1,0:T(8,128)} %bitcast.1, pred[]{:T(512)S(6)} %eq.5), kind=kLoop, calls=%fused_computation | loop fusion | flops 55296 | bytes 442369 | tf_op jit(solution)/shard_map/jit(_where)/select_n | solution.py:350
  1.1 3.7 %collective-permute-start.1 = (f32[3,3,3,8,128]{4,3,2,1,0:T(8,128)S(1)}, f32[3,3,3,8,128]{4,3,2,1,0:T(8,128)S(1)}, u32[]{:S(2)}, u32[]{:S(2)}) collective-permute-start(f32[3,3,3,8,128]{4,3,2,1,0:T(8,128)S(1)} %get-tuple-element.43), channel_id=1, source_target_pairs={{1,2},{3,4},{5,6},{7,8},{9,10},{11,12},{13,14},{2,1},{4,3},{6,5},{... | collective-permute-start | bytes 331784 | tf_op jit(solution)/shard_map/ppermute | solution.py:351
  4.8 1.9 %collective-permute-start = (f32[3,3,3,8,128]{4,3,2,1,0:T(8,128)S(1)}, f32[3,3,3,8,128]{4,3,2,1,0:T(8,128)S(1)}, u32[]{:S(2)}, u32[]{:S(2)}) collective-permute-start(f32[3,3,3,8,128]{4,3,2,1,0:T(8,128)S(1)} %get-tuple-element.44), channel_id=1, source_target_pairs={{0,1},{2,3},{4,5},{6,7},{8,9},{10,11},{12,13},{14,15},{1,0},{3,2},... | collective-permute-start | bytes 331784 | tf_op jit(solution)/shard_map/ppermute | solution.py:352
  6.7 0.5 collective-permute-done.1.side_ref
  7.2 0.8 %collective-permute-done.near_ref = f32[3,3,3,8,128]{4,3,2,1,0:T(8,128)S(1)} collective-permute-done((f32[3,3,3,8,128]{4,3,2,1,0:T(8,128)S(1)}, f32[3,3,3,8,128]{4,3,2,1,0:T(8,128)S(1)}, u32[]{:S(2)}, u32[]{:S(2)}) %collective-permute-start) | collective-permute-done | bytes 110624 | tf_op jit(solution)/shard_map/ppermute | solution.py:352
  8.0 0.5 fine.1
  8.5 12.5 %collective-permute-start.2 = (f32[2,8,128]{2,1,0:T(8,128)S(1)}, f32[2,8,128]{2,1,0:T(8,128)S(1)}, u32[]{:S(2)}, u32[]{:S(2)}) collective-permute-start(f32[2,8,128]{2,1,0:T(8,128)S(1)} %get-tuple-element.24.own_ref), channel_id=1, source_target_pairs={{1,9},{2,10},{3,11},{4,12},{5,13},{6,14},{7,15},{8,0},{9,1},{10,2}... | collective-permute-start | bytes 24584 | tf_op jit(solution)/shard_map/ppermute | solution.py:361
  21.0 0.7 collective-permute-start.3
  22.1 0.7 collective-permute-start.4
  22.7 0.8 %spread.1 = f32[32,3,8,128]{3,2,1,0:T(8,128)} custom-call(f32[3,8,128]{2,1,0:T(8,128)S(1)} %merge.1.column_ref, f32[2,8,128]{2,1,0:T(8,128)S(1)} %collective-permute-done.4.passed_ref), custom_call_target="tpu_custom_call" | custom-call | tf_op jit(solution)/shard_map/spread/pallas_call | solution.py:368
  23.5 17.6 %all-to-all-start = ((f32[32,3,8,128]{3,2,1,0:T(8,128)}), f32[32,3,8,128]{3,2,1,0:T(8,128)S(1)}, u32[]{:S(2)}, u32[]{:S(2)}) async-start(f32[32,3,8,128]{3,2,1,0:T(8,128)} %spread.1), calls=%async_computation | async-start | bytes 786432 | tf_op jit(solution)/shard_map/all_to_all | solution.py:384
  41.1 0.7 collective-permute-start.5
  41.8 7.1 %all-to-all-done.own_ref = f32[32,3,8,128]{3,2,1,0:T(8,128)S(1)} async-done(((f32[32,3,8,128]{3,2,1,0:T(8,128)}), f32[32,3,8,128]{3,2,1,0:T(8,128)S(1)}, u32[]{:S(2)}, u32[]{:S(2)}) %all-to-all-start) | async-done | bytes 393248 | tf_op jit(solution)/shard_map/all_to_all | solution.py:384
  48.9 1.9 %collective-permute-start.6 = (f32[32,3,8,128]{3,2,1,0:T(8,128)S(1)}, f32[32,3,8,128]{3,2,1,0:T(8,128)S(1)}, u32[]{:S(2)}, u32[]{:S(2)}) collective-permute-start(f32[32,3,8,128]{3,2,1,0:T(8,128)S(1)} %all-to-all-done.own_ref), channel_id=1, source_target_pairs={{0,1},{2,3},{4,5},{6,7},{8,9},{10,11},{12,13},{14,15},{1,0},{3,2},... | collective-permute-start | bytes 1179656 | tf_op jit(solution)/shard_map/ppermute | solution.py:387
  50.8 1.7 %collective-permute-done.6.other_ref = f32[32,3,8,128]{3,2,1,0:T(8,128)S(1)} collective-permute-done((f32[32,3,8,128]{3,2,1,0:T(8,128)S(1)}, f32[32,3,8,128]{3,2,1,0:T(8,128)S(1)}, u32[]{:S(2)}, u32[]{:S(2)}) %collective-permute-start.6) | collective-permute-done | bytes 393248 | tf_op jit(solution)/shard_map/ppermute | solution.py:387
  52.5 0.7 collective-permute-start.7
  53.5 0.7 collective-permute-start.9
  54.2 2.1 %collective-permute-start.8 = (f32[3,4,8,128]{3,2,1,0:T(8,128)S(1)}, f32[3,4,8,128]{3,2,1,0:T(8,128)S(1)}, u32[]{:S(2)}, u32[]{:S(2)}) collective-permute-start(f32[3,4,8,128]{3,2,1,0:T(8,128)S(1)} %get-tuple-element.32.end_ref), channel_id=1, source_target_pairs={{0,16},{16,32},{32,48},{48,64},{64,80},{80,96},{96,112},{128,144},... | collective-permute-start | bytes 147464 | tf_op jit(solution)/shard_map/ppermute | solution.py:424
  56.3 4.8 %collective-permute-done.8.prev_ref = f32[3,4,8,128]{3,2,1,0:T(8,128)S(1)} collective-permute-done((f32[3,4,8,128]{3,2,1,0:T(8,128)S(1)}, f32[3,4,8,128]{3,2,1,0:T(8,128)S(1)}, u32[]{:S(2)}, u32[]{:S(2)}) %collective-permute-start.8) | collective-permute-done | bytes 49184 | tf_op jit(solution)/shard_map/ppermute | solution.py:424
  61.2 0.7 collective-permute-start.10
  61.9 1.3 %collective-permute-start.12 = (f32[24,8,128]{2,1,0:T(8,128)S(1)}, f32[24,8,128]{2,1,0:T(8,128)S(1)}, u32[]{:S(2)}, u32[]{:S(2)}) collective-permute-start(f32[24,8,128]{2,1,0:T(8,128)S(1)} %wave.5), channel_id=1, source_target_pairs={{256,385},{258,387},{260,389},{262,391},{264,393},{266,395},{268,3... | collective-permute-start | bytes 294920 | tf_op jit(solution)/shard_map/ppermute | solution.py:429
  63.2 0.7 collective-permute-start.11
  63.9 11.1 %collective-permute-done.12.late_ref = f32[24,8,128]{2,1,0:T(8,128)S(1)} collective-permute-done((f32[24,8,128]{2,1,0:T(8,128)S(1)}, f32[24,8,128]{2,1,0:T(8,128)S(1)}, u32[]{:S(2)}, u32[]{:S(2)}) %collective-permute-start.12) | collective-permute-done | bytes 98336 | tf_op jit(solution)/shard_map/ppermute | solution.py:429
  75.0 1.6 %last.1 = f32[1,3,3,4,8,128]{5,4,3,2,1,0:T(8,128)} custom-call(f32[8,24,8,128]{3,2,1,0:T(8,128)S(1)} %unpack.1.base_ref, f32[24,8,128]{2,1,0:T(8,128)S(1)} %add.12.state_ref, f32[24,8,128]{2,1,0:T(8,128)S(1)} %collective-permute-done.11.given_ref, f32[24,8,128]{2,1,0:T(8,128)S(1)} %collective-permute-done.12.late_ref, f32[3,3,4,8,128]{4,3,2,1,0:T(8,128)S(1)} %bitcast.3, ...), custom_call_target="tpu_custom_call" | custom-call | tf_op jit(solution)/shard_map/last/pallas_call | solution.py:431
  (17 shorter events, 0.8 us)
Async XLA Ops:
  0.0 8.0 %copy-start = (f32[1,3,3,4,8,128]{5,4,3,2,1,0:T(8,128)S(1)}, f32[1,3,3,4,8,128]{5,4,3,2,1,0:T(8,128)}, u32[]{:S(2)}) copy-start(f32[1,3,3,4,8,128]{5,4,3,2,1,0:T(8,128)} %param.1) | copy-start | bytes 442372
  1.1 6.1 %collective-permute-start.1 = (f32[3,3,3,8,128]{4,3,2,1,0:T(8,128)S(1)}, f32[3,3,3,8,128]{4,3,2,1,0:T(8,128)S(1)}, u32[]{:S(2)}, u32[]{:S(2)}) collective-permute-start(f32[3,3,3,8,128]{4,3,2,1,0:T(8,128)S(1)} %get-tuple-element.43), channel_id=1, source_target_pairs={{1,2},{3,4},{5,6},{7,8},{9,10},{11,12},{13,14},{2,1},{4,3},{6,5},{... | collective-permute-start | bytes 331784 | tf_op jit(solution)/shard_map/ppermute | solution.py:351
  4.8 3.2 %collective-permute-start = (f32[3,3,3,8,128]{4,3,2,1,0:T(8,128)S(1)}, f32[3,3,3,8,128]{4,3,2,1,0:T(8,128)S(1)}, u32[]{:S(2)}, u32[]{:S(2)}) collective-permute-start(f32[3,3,3,8,128]{4,3,2,1,0:T(8,128)S(1)} %get-tuple-element.44), channel_id=1, source_target_pairs={{0,1},{2,3},{4,5},{6,7},{8,9},{10,11},{12,13},{14,15},{1,0},{3,2},... | collective-permute-start | bytes 331784 | tf_op jit(solution)/shard_map/ppermute | solution.py:352
  8.5 13.6 %collective-permute-start.2 = (f32[2,8,128]{2,1,0:T(8,128)S(1)}, f32[2,8,128]{2,1,0:T(8,128)S(1)}, u32[]{:S(2)}, u32[]{:S(2)}) collective-permute-start(f32[2,8,128]{2,1,0:T(8,128)S(1)} %get-tuple-element.24.own_ref), channel_id=1, source_target_pairs={{1,9},{2,10},{3,11},{4,12},{5,13},{6,14},{7,15},{8,0},{9,1},{10,2}... | collective-permute-start | bytes 24584 | tf_op jit(solution)/shard_map/ppermute | solution.py:361
  21.0 1.0 %collective-permute-start.3 = (f32[2,8,128]{2,1,0:T(8,128)S(1)}, f32[2,8,128]{2,1,0:T(8,128)S(1)}, u32[]{:S(2)}, u32[]{:S(2)}) collective-permute-start(f32[2,8,128]{2,1,0:T(8,128)S(1)} %get-tuple-element.24.own_ref), channel_id=1, source_target_pairs={{0,9},{16,25},{32,41},{48,57},{64,73},{80,89},{96,105},{112,121},{... | collective-permute-start | bytes 24584 | tf_op jit(solution)/shard_map/ppermute | solution.py:362
  22.1 0.7 collective-permute-start.4
  23.5 25.4 %all-to-all-start = ((f32[32,3,8,128]{3,2,1,0:T(8,128)}), f32[32,3,8,128]{3,2,1,0:T(8,128)S(1)}, u32[]{:S(2)}, u32[]{:S(2)}) async-start(f32[32,3,8,128]{3,2,1,0:T(8,128)} %spread.1), calls=%async_computation | async-start | bytes 786432 | tf_op jit(solution)/shard_map/all_to_all | solution.py:384
  41.1 0.7 collective-permute-start.5
  48.9 3.6 %collective-permute-start.6 = (f32[32,3,8,128]{3,2,1,0:T(8,128)S(1)}, f32[32,3,8,128]{3,2,1,0:T(8,128)S(1)}, u32[]{:S(2)}, u32[]{:S(2)}) collective-permute-start(f32[32,3,8,128]{3,2,1,0:T(8,128)S(1)} %all-to-all-done.own_ref), channel_id=1, source_target_pairs={{0,1},{2,3},{4,5},{6,7},{8,9},{10,11},{12,13},{14,15},{1,0},{3,2},... | collective-permute-start | bytes 1179656 | tf_op jit(solution)/shard_map/ppermute | solution.py:387
  52.5 1.0 %collective-permute-start.7 = (f32[24,8,128]{2,1,0:T(8,128)S(1)}, f32[24,8,128]{2,1,0:T(8,128)S(1)}, u32[]{:S(2)}, u32[]{:S(2)}) collective-permute-start(f32[24,8,128]{2,1,0:T(8,128)S(1)} %wave.3), channel_id=1, source_target_pairs={{0,128},{2,130},{4,132},{6,134},{8,136},{10,138},{12,140},{14,142}... | collective-permute-start | bytes 294920 | tf_op jit(solution)/shard_map/ppermute | solution.py:411
  53.5 7.6 %collective-permute-start.9 = (f32[24,8,128]{2,1,0:T(8,128)S(1)}, f32[24,8,128]{2,1,0:T(8,128)S(1)}, u32[]{:S(2)}, u32[]{:S(2)}) collective-permute-start(f32[24,8,128]{2,1,0:T(8,128)S(1)} %wave.4), channel_id=1, source_target_pairs={{128,256},{130,258},{132,260},{134,262},{136,264},{138,266},{140,2... | collective-permute-start | bytes 294920 | tf_op jit(solution)/shard_map/ppermute | solution.py:425
  54.2 6.9 %collective-permute-start.8 = (f32[3,4,8,128]{3,2,1,0:T(8,128)S(1)}, f32[3,4,8,128]{3,2,1,0:T(8,128)S(1)}, u32[]{:S(2)}, u32[]{:S(2)}) collective-permute-start(f32[3,4,8,128]{3,2,1,0:T(8,128)S(1)} %get-tuple-element.32.end_ref), channel_id=1, source_target_pairs={{0,16},{16,32},{32,48},{48,64},{64,80},{80,96},{96,112},{128,144},... | collective-permute-start | bytes 147464 | tf_op jit(solution)/shard_map/ppermute | solution.py:424
  61.2 2.7 %collective-permute-start.10 = (f32[24,8,128]{2,1,0:T(8,128)S(1)}, f32[24,8,128]{2,1,0:T(8,128)S(1)}, u32[]{:S(2)}, u32[]{:S(2)}) collective-permute-start(f32[24,8,128]{2,1,0:T(8,128)S(1)} %wave.5), channel_id=1, source_target_pairs={{256,384},{258,386},{260,388},{262,390},{264,392},{266,394},{268,3... | collective-permute-start | bytes 294920 | tf_op jit(solution)/shard_map/ppermute | solution.py:425
  61.9 13.1 %collective-permute-start.12 = (f32[24,8,128]{2,1,0:T(8,128)S(1)}, f32[24,8,128]{2,1,0:T(8,128)S(1)}, u32[]{:S(2)}, u32[]{:S(2)}) collective-permute-start(f32[24,8,128]{2,1,0:T(8,128)S(1)} %wave.5), channel_id=1, source_target_pairs={{256,385},{258,387},{260,389},{262,391},{264,393},{266,395},{268,3... | collective-permute-start | bytes 294920 | tf_op jit(solution)/shard_map/ppermute | solution.py:429
  63.2 11.8 %collective-permute-start.11 = (f32[24,8,128]{2,1,0:T(8,128)S(1)}, f32[24,8,128]{2,1,0:T(8,128)S(1)}, u32[]{:S(2)}, u32[]{:S(2)}) collective-permute-start(f32[24,8,128]{2,1,0:T(8,128)S(1)} %add.11.state_ref), channel_id=1, source_target_pairs={{128,129},{130,131},{132,133},{134,135},{136,137},{138,139},{140,1... | collective-permute-start | bytes 294920 | tf_op jit(solution)/shard_map/ppermute | solution.py:430

commit v2 on v1

--- a/solution.py
+++ b/solution.py
@@ -66,7 +66,7 @@
     return total * 0.125
 
 
-def fine_kernel(near_ref, side_ref, nodes_ref, mid_ref, end_ref, start_c_ref, end_c_ref, packed_ref):
+def fine_kernel(near_ref, side_ref, nodes_ref, mid_ref, end_ref, start_c_ref, end_c_ref, packed_ref, again_ref):
     here = lax.axis_index("space")
     last = lax.axis_size("space") - 1
     even = here % 2 == 0
@@ -142,16 +142,15 @@
         place == 0, planes[0], jnp.where(place == 1, planes[1], jnp.where(place == 2, planes[2], planes[3]))
     )
     packed_ref[1] = jnp.where(place == 0, planes[4], jnp.where(place == 1, planes[5], 0.0))
-
-
-def merge_kernel(own_ref, other_ref, column_ref):
-    column_ref[0] = own_ref[0]
-    column_ref[1] = other_ref[0]
-    column_ref[2] = own_ref[1] + other_ref[1]
-
-
-def spread_kernel(column_ref, passed_ref, copies_ref):
-    tiles = column_ref[0], column_ref[1] + passed_ref[0], column_ref[2] + passed_ref[1]
+    for n in range(2, packed_ref.shape[0]):
+        packed_ref[n] = jnp.zeros((8, 128), jnp.float32)
+    again_ref[0] = packed_ref[0]
+    again_ref[1] = packed_ref[1]
+
+
+def spread_kernel(own_ref, across_ref, passed_ref, copies_ref):
+    other = [across_ref[n] + passed_ref[n] for n in range(2)]
+    tiles = own_ref[0], other[0], own_ref[1] + other[1]
     for i in range(copies_ref.shape[0]):
         for n in range(3):
             copies_ref[i, n] = tiles[n]
@@ -350,29 +349,25 @@
     to_side = jnp.where(even, bottom, top)
     side = lax.ppermute(to_side, "space", swaps([(i, i + 1) for i in range(1, slabs - 1, 2)]))
     near = lax.ppermute(jnp.where(even, top, bottom), "space", swaps([(i, i + 1) for i in range(0, slabs, 2)]))
-    mid, end, start_c, end_c, packed = pl.pallas_call(
+    mid, end, start_c, end_c, packed, again = pl.pallas_call(
         fine_kernel,
-        out_shape=[shape(3, 4), shape(3, 4), shape(3, 2), shape(3, 2), shape(2)],
+        out_shape=[shape(3, 4), shape(3, 4), shape(3, 2), shape(3, 2), shape(4), shape(2)],
         in_specs=vmem(3),
-        out_specs=vmem(5),
+        out_specs=vmem(6),
         compiler_params=PARAMS,
         name="fine",
     )(near, side, nodes)
     across = lax.ppermute(packed, "space", [(i, (i + middle) % slabs) for i in range(1, slabs)])
-    beside = lax.ppermute(packed, "space", [(0, middle + 1)])
-    column = pl.pallas_call(
-        merge_kernel, out_shape=shape(3), in_specs=vmem(2), out_specs=vmem(1)[0], compiler_params=PARAMS, name="merge"
-    )(packed, across)
-    column, beside = lax.optimization_barrier((column, beside))
+    beside = lax.ppermute(again, "space", [(0, middle + 1)])
     passed = lax.ppermute(beside, "space", [(middle + 1, middle)])
     copies = pl.pallas_call(
         spread_kernel,
         out_shape=shape(32, 3),
-        in_specs=vmem(2),
+        in_specs=vmem(3),
         out_specs=vmem(1)[0],
         compiler_params=PARAMS,
         name="spread",
-    )(column, passed)
+    )(packed, across, passed)
 
     device = lambda zl, y, zh, x, core: (zl * 4 + y) * slabs + zh * 8 + x * 2 + core
     layers = [

time: 77 us -> 76.5 us (level)
  transfers between devices with their start and end apart: 14 -> 14, of which waited for: 7 -> 6; matrix products, arithmetic and copies ran while one was open for 0% -> 0% of each run, Pallas kernels for 0% -> 0%
where the time goes in v2:
time: 76.5 us; the launch traced here: 76 us
  starting transfers between devices  45.5 us (59%)
  waiting for transfers between devices  26 us (34%)
  Pallas kernels  3.22 us (4%)
  other arithmetic  1.09 us (1%)
    all_to_all x1, starting transfers between devices, local(): own = lax.all_to_all(copies, both, 0, 0, axis_index_groups=layers)  17.4 us
    ppermute x1, starting transfers between devices, local(): lax.ppermute(packed, 'space', [(i, (i + middle) % slabs) for i in range(1...  12.5 us
    ppermute x1, waiting for transfers between devices, local(): lax.ppermute(after, both, [(i, i + count * slabs + 1) for i in cores([GRO...  11.2 us
    all_to_all x1, waiting for transfers between devices, local(): own = lax.all_to_all(copies, both, 0, 0, axis_index_groups=layers)  7.08 us
    ppermute x1, waiting for transfers between devices, local(): lax.ppermute(handed, 'tm', [(i, i + 1) for i in range(slices - 1) if i +...  4.82 us
    ppermute x1, starting transfers between devices, local(): lax.ppermute(to_side, 'space', swaps([(i, i + 1) for i in range(1, slabs...  3.68 us
    ppermute x1, starting transfers between devices, local(): lax.ppermute(handed, 'tm', [(i, i + 1) for i in range(slices - 1) if i +...  2.12 us
    ppermute x1, starting transfers between devices, local(): lax.ppermute(jnp.where(even, top, bottom), 'space', swaps([(i, i + 1) for...  1.92 us
  transfers between devices with their start and end apart: 14, of which 6 were waited for; matrix products, arithmetic and copies ran while one was open for 0% of the time, Pallas kernels for 0%

profile of v2, /device:TPU:225, one launch (start us, length us, event | category | flops | bytes accessed | tf_op | source)
XLA Modules:
  0.0 76.0 jit_solution(4458171143717433971)
XLA Ops:
  0.0 1.1 %slice_select_fusion = (f32[3,3,3,8,128]{4,3,2,1,0:T(8,128)S(1)}, f32[3,3,3,8,128]{4,3,2,1,0:T(8,128)S(1)}) fusion(f32[3,3,4,8,128]{4,3,2,1,0:T(8,128)} %bitcast.1, pred[]{:T(512)S(6)} %eq.5), kind=kLoop, calls=%fused_computation | loop fusion | flops 55296 | bytes 442369 | tf_op jit(solution)/shard_map/jit(_where)/select_n | solution.py:349
  1.1 3.7 %collective-permute-start.1 = (f32[3,3,3,8,128]{4,3,2,1,0:T(8,128)S(1)}, f32[3,3,3,8,128]{4,3,2,1,0:T(8,128)S(1)}, u32[]{:S(2)}, u32[]{:S(2)}) collective-permute-start(f32[3,3,3,8,128]{4,3,2,1,0:T(8,128)S(1)} %get-tuple-element.41), channel_id=1, source_target_pairs={{1,2},{3,4},{5,6},{7,8},{9,10},{11,12},{13,14},{2,1},{4,3},{6,5},{... | collective-permute-start | bytes 331784 | tf_op jit(solution)/shard_map/ppermute | solution.py:350
  4.8 1.9 %collective-permute-start = (f32[3,3,3,8,128]{4,3,2,1,0:T(8,128)S(1)}, f32[3,3,3,8,128]{4,3,2,1,0:T(8,128)S(1)}, u32[]{:S(2)}, u32[]{:S(2)}) collective-permute-start(f32[3,3,3,8,128]{4,3,2,1,0:T(8,128)S(1)} %get-tuple-element.42), channel_id=1, source_target_pairs={{0,1},{2,3},{4,5},{6,7},{8,9},{10,11},{12,13},{14,15},{1,0},{3,2},... | collective-permute-start | bytes 331784 | tf_op jit(solution)/shard_map/ppermute | solution.py:351
  6.7 0.5 collective-permute-done.1.side_ref
  7.2 0.8 %collective-permute-done.near_ref = f32[3,3,3,8,128]{4,3,2,1,0:T(8,128)S(1)} collective-permute-done((f32[3,3,3,8,128]{4,3,2,1,0:T(8,128)S(1)}, f32[3,3,3,8,128]{4,3,2,1,0:T(8,128)S(1)}, u32[]{:S(2)}, u32[]{:S(2)}) %collective-permute-start) | collective-permute-done | bytes 110624 | tf_op jit(solution)/shard_map/ppermute | solution.py:351
  8.0 0.5 fine.1
  8.5 12.5 %collective-permute-start.2 = (f32[4,8,128]{2,1,0:T(8,128)S(1)}, f32[4,8,128]{2,1,0:T(8,128)S(1)}, u32[]{:S(2)}, u32[]{:S(2)}) collective-permute-start(f32[4,8,128]{2,1,0:T(8,128)S(1)} %get-tuple-element.23.own_ref), channel_id=1, source_target_pairs={{1,9},{2,10},{3,11},{4,12},{5,13},{6,14},{7,15},{8,0},{9,1},{10,2}... | collective-permute-start | bytes 49160 | tf_op jit(solution)/shard_map/ppermute | solution.py:360
  21.0 0.7 collective-permute-start.3
  21.7 0.7 collective-permute-start.4
  22.4 0.8 %spread.1 = f32[32,3,8,128]{3,2,1,0:T(8,128)} custom-call(f32[4,8,128]{2,1,0:T(8,128)S(1)} %get-tuple-element.23.own_ref, f32[4,8,128]{2,1,0:T(8,128)S(1)} %collective-permute-done.2.across_ref, f32[2,8,128]{2,1,0:T(8,128)S(1)} %collective-permute-done.4.passed_ref), custom_call_target="tpu_custom_call" | custom-call | tf_op jit(solution)/shard_map/spread/pallas_call | solution.py:363
  23.2 17.4 %all-to-all-start = ((f32[32,3,8,128]{3,2,1,0:T(8,128)}), f32[32,3,8,128]{3,2,1,0:T(8,128)S(1)}, u32[]{:S(2)}, u32[]{:S(2)}) async-start(f32[32,3,8,128]{3,2,1,0:T(8,128)} %spread.1), calls=%async_computation | async-start | bytes 786432 | tf_op jit(solution)/shard_map/all_to_all | solution.py:379
  40.6 0.7 collective-permute-start.5
  41.2 7.1 %all-to-all-done.own_ref = f32[32,3,8,128]{3,2,1,0:T(8,128)S(1)} async-done(((f32[32,3,8,128]{3,2,1,0:T(8,128)}), f32[32,3,8,128]{3,2,1,0:T(8,128)S(1)}, u32[]{:S(2)}, u32[]{:S(2)}) %all-to-all-start) | async-done | bytes 393248 | tf_op jit(solution)/shard_map/all_to_all | solution.py:379
  48.3 1.9 %collective-permute-start.6 = (f32[32,3,8,128]{3,2,1,0:T(8,128)S(1)}, f32[32,3,8,128]{3,2,1,0:T(8,128)S(1)}, u32[]{:S(2)}, u32[]{:S(2)}) collective-permute-start(f32[32,3,8,128]{3,2,1,0:T(8,128)S(1)} %all-to-all-done.own_ref), channel_id=1, source_target_pairs={{0,1},{2,3},{4,5},{6,7},{8,9},{10,11},{12,13},{14,15},{1,0},{3,2},... | collective-permute-start | bytes 1179656 | tf_op jit(solution)/shard_map/ppermute | solution.py:382
  50.2 1.7 %collective-permute-done.6.other_ref = f32[32,3,8,128]{3,2,1,0:T(8,128)S(1)} collective-permute-done((f32[32,3,8,128]{3,2,1,0:T(8,128)S(1)}, f32[32,3,8,128]{3,2,1,0:T(8,128)S(1)}, u32[]{:S(2)}, u32[]{:S(2)}) %collective-permute-start.6) | collective-permute-done | bytes 393248 | tf_op jit(solution)/shard_map/ppermute | solution.py:382
  51.9 0.7 collective-permute-start.7
  52.9 0.7 collective-permute-start.9
  53.6 2.1 %collective-permute-start.8 = (f32[3,4,8,128]{3,2,1,0:T(8,128)S(1)}, f32[3,4,8,128]{3,2,1,0:T(8,128)S(1)}, u32[]{:S(2)}, u32[]{:S(2)}) collective-permute-start(f32[3,4,8,128]{3,2,1,0:T(8,128)S(1)} %get-tuple-element.30.end_ref), channel_id=1, source_target_pairs={{0,16},{16,32},{32,48},{48,64},{64,80},{80,96},{96,112},{128,144},... | collective-permute-start | bytes 147464 | tf_op jit(solution)/shard_map/ppermute | solution.py:419
  55.7 4.8 %collective-permute-done.8.prev_ref = f32[3,4,8,128]{3,2,1,0:T(8,128)S(1)} collective-permute-done((f32[3,4,8,128]{3,2,1,0:T(8,128)S(1)}, f32[3,4,8,128]{3,2,1,0:T(8,128)S(1)}, u32[]{:S(2)}, u32[]{:S(2)}) %collective-permute-start.8) | collective-permute-done | bytes 49184 | tf_op jit(solution)/shard_map/ppermute | solution.py:419
  60.6 0.7 collective-permute-start.10
  61.3 1.3 %collective-permute-start.12 = (f32[24,8,128]{2,1,0:T(8,128)S(1)}, f32[24,8,128]{2,1,0:T(8,128)S(1)}, u32[]{:S(2)}, u32[]{:S(2)}) collective-permute-start(f32[24,8,128]{2,1,0:T(8,128)S(1)} %wave.5), channel_id=1, source_target_pairs={{256,385},{258,387},{260,389},{262,391},{264,393},{266,395},{268,3... | collective-permute-start | bytes 294920 | tf_op jit(solution)/shard_map/ppermute | solution.py:424
  62.6 0.7 collective-permute-start.11
  63.3 11.2 %collective-permute-done.12.late_ref = f32[24,8,128]{2,1,0:T(8,128)S(1)} collective-permute-done((f32[24,8,128]{2,1,0:T(8,128)S(1)}, f32[24,8,128]{2,1,0:T(8,128)S(1)}, u32[]{:S(2)}, u32[]{:S(2)}) %collective-permute-start.12) | collective-permute-done | bytes 98336 | tf_op jit(solution)/shard_map/ppermute | solution.py:424
  74.4 1.6 %last.1 = f32[1,3,3,4,8,128]{5,4,3,2,1,0:T(8,128)} custom-call(f32[8,24,8,128]{3,2,1,0:T(8,128)S(1)} %unpack.1.base_ref, f32[24,8,128]{2,1,0:T(8,128)S(1)} %add.12.state_ref, f32[24,8,128]{2,1,0:T(8,128)S(1)} %collective-permute-done.11.given_ref, f32[24,8,128]{2,1,0:T(8,128)S(1)} %collective-permute-done.12.late_ref, f32[3,3,4,8,128]{4,3,2,1,0:T(8,128)S(1)} %bitcast.3, ...), custom_call_target="tpu_custom_call" | custom-call | tf_op jit(solution)/shard_map/last/pallas_call | solution.py:426
  (16 shorter events, 0.4 us)
Async XLA Ops:
  0.0 8.0 %copy-start = (f32[1,3,3,4,8,128]{5,4,3,2,1,0:T(8,128)S(1)}, f32[1,3,3,4,8,128]{5,4,3,2,1,0:T(8,128)}, u32[]{:S(2)}) copy-start(f32[1,3,3,4,8,128]{5,4,3,2,1,0:T(8,128)} %param.1) | copy-start | bytes 442372
  1.1 6.1 %collective-permute-start.1 = (f32[3,3,3,8,128]{4,3,2,1,0:T(8,128)S(1)}, f32[3,3,3,8,128]{4,3,2,1,0:T(8,128)S(1)}, u32[]{:S(2)}, u32[]{:S(2)}) collective-permute-start(f32[3,3,3,8,128]{4,3,2,1,0:T(8,128)S(1)} %get-tuple-element.41), channel_id=1, source_target_pairs={{1,2},{3,4},{5,6},{7,8},{9,10},{11,12},{13,14},{2,1},{4,3},{6,5},{... | collective-permute-start | bytes 331784 | tf_op jit(solution)/shard_map/ppermute | solution.py:350
  4.8 3.2 %collective-permute-start = (f32[3,3,3,8,128]{4,3,2,1,0:T(8,128)S(1)}, f32[3,3,3,8,128]{4,3,2,1,0:T(8,128)S(1)}, u32[]{:S(2)}, u32[]{:S(2)}) collective-permute-start(f32[3,3,3,8,128]{4,3,2,1,0:T(8,128)S(1)} %get-tuple-element.42), channel_id=1, source_target_pairs={{0,1},{2,3},{4,5},{6,7},{8,9},{10,11},{12,13},{14,15},{1,0},{3,2},... | collective-permute-start | bytes 331784 | tf_op jit(solution)/shard_map/ppermute | solution.py:351
  8.5 13.9 %collective-permute-start.2 = (f32[4,8,128]{2,1,0:T(8,128)S(1)}, f32[4,8,128]{2,1,0:T(8,128)S(1)}, u32[]{:S(2)}, u32[]{:S(2)}) collective-permute-start(f32[4,8,128]{2,1,0:T(8,128)S(1)} %get-tuple-element.23.own_ref), channel_id=1, source_target_pairs={{1,9},{2,10},{3,11},{4,12},{5,13},{6,14},{7,15},{8,0},{9,1},{10,2}... | collective-permute-start | bytes 49160 | tf_op jit(solution)/shard_map/ppermute | solution.py:360
  21.0 0.7 collective-permute-start.3
  21.7 0.7 collective-permute-start.4
  23.2 25.1 %all-to-all-start = ((f32[32,3,8,128]{3,2,1,0:T(8,128)}), f32[32,3,8,128]{3,2,1,0:T(8,128)S(1)}, u32[]{:S(2)}, u32[]{:S(2)}) async-start(f32[32,3,8,128]{3,2,1,0:T(8,128)} %spread.1), calls=%async_computation | async-start | bytes 786432 | tf_op jit(solution)/shard_map/all_to_all | solution.py:379
  40.6 0.7 collective-permute-start.5
  48.3 3.6 %collective-permute-start.6 = (f32[32,3,8,128]{3,2,1,0:T(8,128)S(1)}, f32[32,3,8,128]{3,2,1,0:T(8,128)S(1)}, u32[]{:S(2)}, u32[]{:S(2)}) collective-permute-start(f32[32,3,8,128]{3,2,1,0:T(8,128)S(1)} %all-to-all-done.own_ref), channel_id=1, source_target_pairs={{0,1},{2,3},{4,5},{6,7},{8,9},{10,11},{12,13},{14,15},{1,0},{3,2},... | collective-permute-start | bytes 1179656 | tf_op jit(solution)/shard_map/ppermute | solution.py:382
  51.9 1.0 %collective-permute-start.7 = (f32[24,8,128]{2,1,0:T(8,128)S(1)}, f32[24,8,128]{2,1,0:T(8,128)S(1)}, u32[]{:S(2)}, u32[]{:S(2)}) collective-permute-start(f32[24,8,128]{2,1,0:T(8,128)S(1)} %wave.3), channel_id=1, source_target_pairs={{0,128},{2,130},{4,132},{6,134},{8,136},{10,138},{12,140},{14,142}... | collective-permute-start | bytes 294920 | tf_op jit(solution)/shard_map/ppermute | solution.py:406
  52.9 7.6 %collective-permute-start.9 = (f32[24,8,128]{2,1,0:T(8,128)S(1)}, f32[24,8,128]{2,1,0:T(8,128)S(1)}, u32[]{:S(2)}, u32[]{:S(2)}) collective-permute-start(f32[24,8,128]{2,1,0:T(8,128)S(1)} %wave.4), channel_id=1, source_target_pairs={{128,256},{130,258},{132,260},{134,262},{136,264},{138,266},{140,2... | collective-permute-start | bytes 294920 | tf_op jit(solution)/shard_map/ppermute | solution.py:420
  53.6 6.9 %collective-permute-start.8 = (f32[3,4,8,128]{3,2,1,0:T(8,128)S(1)}, f32[3,4,8,128]{3,2,1,0:T(8,128)S(1)}, u32[]{:S(2)}, u32[]{:S(2)}) collective-permute-start(f32[3,4,8,128]{3,2,1,0:T(8,128)S(1)} %get-tuple-element.30.end_ref), channel_id=1, source_target_pairs={{0,16},{16,32},{32,48},{48,64},{64,80},{80,96},{96,112},{128,144},... | collective-permute-start | bytes 147464 | tf_op jit(solution)/shard_map/ppermute | solution.py:419
  60.6 2.7 %collective-permute-start.10 = (f32[24,8,128]{2,1,0:T(8,128)S(1)}, f32[24,8,128]{2,1,0:T(8,128)S(1)}, u32[]{:S(2)}, u32[]{:S(2)}) collective-permute-start(f32[24,8,128]{2,1,0:T(8,128)S(1)} %wave.5), channel_id=1, source_target_pairs={{256,384},{258,386},{260,388},{262,390},{264,392},{266,394},{268,3... | collective-permute-start | bytes 294920 | tf_op jit(solution)/shard_map/ppermute | solution.py:420
  61.3 13.2 %collective-permute-start.12 = (f32[24,8,128]{2,1,0:T(8,128)S(1)}, f32[24,8,128]{2,1,0:T(8,128)S(1)}, u32[]{:S(2)}, u32[]{:S(2)}) collective-permute-start(f32[24,8,128]{2,1,0:T(8,128)S(1)} %wave.5), channel_id=1, source_target_pairs={{256,385},{258,387},{260,389},{262,391},{264,393},{266,395},{268,3... | collective-permute-start | bytes 294920 | tf_op jit(solution)/shard_map/ppermute | solution.py:424
  62.6 11.9 %collective-permute-start.11 = (f32[24,8,128]{2,1,0:T(8,128)S(1)}, f32[24,8,128]{2,1,0:T(8,128)S(1)}, u32[]{:S(2)}, u32[]{:S(2)}) collective-permute-start(f32[24,8,128]{2,1,0:T(8,128)S(1)} %add.11.state_ref), channel_id=1, source_target_pairs={{128,129},{130,131},{132,133},{134,135},{136,137},{138,139},{140,1... | collective-permute-start | bytes 294920 | tf_op jit(solution)/shard_map/ppermute | solution.py:425

commit v3 on v2

--- a/solution.py
+++ b/solution.py
@@ -240,7 +240,9 @@
 
 
 def runs_wave(wave, count):
-    return (lax.axis_index("tm") // count == wave) & (lax.axis_index("space") % 2 == 0)
+    slice_id = lax.axis_index("tm")
+    runs = (slice_id // count == wave) & (lax.axis_index("space") % 2 == 0)
+    return runs if wave == GROUPS - 2 else runs & (slice_id % count >= count // 2)
 
 
 def first_wave_kernel(count, own_ref, other_ref, out_ref):
@@ -382,8 +384,14 @@
     other = lax.ppermute(own, "space", swaps([(i, i + 1) for i in range(0, slabs, 2)]))
     count = slices // GROUPS
 
-    def cores(groups):
-        return [((g * count + i) * slabs + s) for g in groups for i in range(count) for s in range(0, slabs, 2)]
+    def cores(groups, begin=0):
+        return [((g * count + i) * slabs + s) for g in groups for i in range(begin, count) for s in range(0, slabs, 2)]
+
+    def handed_on(after, wave):
+        senders = cores([wave], count // 2)
+        upper = lax.ppermute(after, both, [(i, i + count * slabs) for i in senders])
+        lower = lax.ppermute(after, both, [(i, i + count // 2 * slabs) for i in senders])
+        return upper, lower
 
     after = pl.pallas_call(
         functools.partial(first_wave_kernel, count),
@@ -403,7 +411,8 @@
         cost_estimate=pl.CostEstimate(flops=10_000_000, bytes_accessed=10_000_000, transcendentals=0),
         name="unpack",
     )(own, other)
-    state = lax.ppermute(after, both, [(i, i + count * slabs) for i in cores([0])])
+    upper, lower = handed_on(after, 0)
+    state = lower + upper
     for wave in range(1, GROUPS - 1):
         after = pl.pallas_call(
             functools.partial(wave_kernel, wave, count),
@@ -417,10 +426,12 @@
         if wave == 1:
             handed, after = lax.optimization_barrier((end, after))
             prev = lax.ppermute(handed, "tm", [(i, i + 1) for i in range(slices - 1) if i + 1 not in CORNERS])
-        moved = lax.ppermute(after, both, [(i, i + count * slabs) for i in cores([wave])])
-        if wave == 1:
-            prev, moved = lax.optimization_barrier((prev, moved))
-        state = moved + early
+        if wave < GROUPS - 2:
+            upper, lower = handed_on(after, wave)
+            prev, lower, upper = lax.optimization_barrier((prev, lower, upper))
+            state = lower + upper + early
+        else:
+            state = lax.ppermute(after, both, [(i, i + count * slabs) for i in cores([wave])]) + early
     late = lax.ppermute(after, both, [(i, i + count * slabs + 1) for i in cores([GROUPS - 2])])
     given = lax.ppermute(early, both, [(i, i + 1) for i in cores(range(1, GROUPS - 1))])
     return pl.pallas_call(

time: 76.5 us -> 76.9 us (level)
  the two profiles are of different devices: /device:TPU:225 before, /device:TPU:32 now
where the time goes in v3:
time: 76.9 us; the launch traced here: 76.5 us
  starting transfers between devices  40 us (52%)
  waiting for transfers between devices  30.9 us (40%)
  Pallas kernels  4.24 us (6%)
  other arithmetic  1.1 us (1%)
    ppermute x1, starting transfers between devices, local(): beside = lax.ppermute(again, 'space', [(0, middle + 1)])  15.4 us
    ppermute x1, waiting for transfers between devices, local(): lax.ppermute(packed, 'space', [(i, (i + middle) % slabs) for i in range(1...  11.3 us
    all_to_all x1, waiting for transfers between devices, local(): own = lax.all_to_all(copies, both, 0, 0, axis_index_groups=layers)  7.95 us
    all_to_all x1, starting transfers between devices, local(): own = lax.all_to_all(copies, both, 0, 0, axis_index_groups=layers)  6.09 us
    ppermute x1, waiting for transfers between devices, local(): lax.ppermute(handed, 'tm', [(i, i + 1) for i in range(slices - 1) if i +...  5.72 us
    ppermute x1, starting transfers between devices, local(): lax.ppermute(jnp.where(even, top, bottom), 'space', swaps([(i, i + 1) for...  4.76 us
    ppermute x1, starting transfers between devices, local(): lax.ppermute(handed, 'tm', [(i, i + 1) for i in range(slices - 1) if i +...  2.37 us
    ppermute x2, starting transfers between devices, handed_on(): upper = lax.ppermute(after, both, [(i, i + count * slabs) for i in senders])  2.23 us
  transfers between devices with their start and end apart: 16, of which 8 were waited for; matrix products, arithmetic and copies ran while one was open for 0% of the time, Pallas kernels for 0%

profile of v3, /device:TPU:32, one launch (start us, length us, event | category | flops | bytes accessed | tf_op | source)
XLA Modules:
  0.0 76.5 jit_solution(13901534729803896072)
XLA Ops:
  0.0 1.1 %slice_select_fusion = (f32[3,3,3,8,128]{4,3,2,1,0:T(8,128)S(1)}, f32[3,3,3,8,128]{4,3,2,1,0:T(8,128)S(1)}) fusion(f32[3,3,4,8,128]{4,3,2,1,0:T(8,128)} %bitcast.1, pred[]{:T(512)S(6)} %eq.5), kind=kLoop, calls=%fused_computation | loop fusion | flops 55296 | bytes 442369 | tf_op jit(solution)/shard_map/jit(_where)/select_n | solution.py:351
  1.1 0.7 collective-permute-start.1
  1.7 4.8 %collective-permute-start = (f32[3,3,3,8,128]{4,3,2,1,0:T(8,128)S(1)}, f32[3,3,3,8,128]{4,3,2,1,0:T(8,128)S(1)}, u32[]{:S(2)}, u32[]{:S(2)}) collective-permute-start(f32[3,3,3,8,128]{4,3,2,1,0:T(8,128)S(1)} %get-tuple-element.44), channel_id=1, source_target_pairs={{0,1},{2,3},{4,5},{6,7},{8,9},{10,11},{12,13},{14,15},{1,0},{3,2},... | collective-permute-start | bytes 331784 | tf_op jit(solution)/shard_map/ppermute | solution.py:353
  6.5 0.9 %collective-permute-done.near_ref = f32[3,3,3,8,128]{4,3,2,1,0:T(8,128)S(1)} collective-permute-done((f32[3,3,3,8,128]{4,3,2,1,0:T(8,128)S(1)}, f32[3,3,3,8,128]{4,3,2,1,0:T(8,128)S(1)}, u32[]{:S(2)}, u32[]{:S(2)}) %collective-permute-start) | collective-permute-done | bytes 110624 | tf_op jit(solution)/shard_map/ppermute | solution.py:353
  7.9 1.3 %collective-permute-start.2 = (f32[4,8,128]{2,1,0:T(8,128)S(1)}, f32[4,8,128]{2,1,0:T(8,128)S(1)}, u32[]{:S(2)}, u32[]{:S(2)}) collective-permute-start(f32[4,8,128]{2,1,0:T(8,128)S(1)} %get-tuple-element.24.own_ref), channel_id=1, source_target_pairs={{1,9},{2,10},{3,11},{4,12},{5,13},{6,14},{7,15},{8,0},{9,1},{10,2}... | collective-permute-start | bytes 49160 | tf_op jit(solution)/shard_map/ppermute | solution.py:362
  9.2 15.4 %collective-permute-start.3 = (f32[2,8,128]{2,1,0:T(8,128)S(1)}, f32[2,8,128]{2,1,0:T(8,128)S(1)}, u32[]{:S(2)}, u32[]{:S(2)}) collective-permute-start(f32[2,8,128]{2,1,0:T(8,128)S(1)} %get-tuple-element.25), channel_id=1, source_target_pairs={{0,9},{16,25},{32,41},{48,57},{64,73},{80,89},{96,105},{112,121},{... | collective-permute-start | bytes 24584 | tf_op jit(solution)/shard_map/ppermute | solution.py:363
  24.7 1.3 %collective-permute-done.3 = f32[2,8,128]{2,1,0:T(8,128)S(1)} collective-permute-done((f32[2,8,128]{2,1,0:T(8,128)S(1)}, f32[2,8,128]{2,1,0:T(8,128)S(1)}, u32[]{:S(2)}, u32[]{:S(2)}) %collective-permute-start.3) | collective-permute-done | bytes 8224 | tf_op jit(solution)/shard_map/ppermute | solution.py:363
  26.7 11.3 %collective-permute-done.2.across_ref = f32[4,8,128]{2,1,0:T(8,128)S(1)} collective-permute-done((f32[4,8,128]{2,1,0:T(8,128)S(1)}, f32[4,8,128]{2,1,0:T(8,128)S(1)}, u32[]{:S(2)}, u32[]{:S(2)}) %collective-permute-start.2) | collective-permute-done | bytes 16416 | tf_op jit(solution)/shard_map/ppermute | solution.py:362
  38.0 0.8 %spread.1 = f32[32,3,8,128]{3,2,1,0:T(8,128)} custom-call(f32[4,8,128]{2,1,0:T(8,128)S(1)} %get-tuple-element.24.own_ref, f32[4,8,128]{2,1,0:T(8,128)S(1)} %collective-permute-done.2.across_ref, f32[2,8,128]{2,1,0:T(8,128)S(1)} %collective-permute-done.4.passed_ref), custom_call_target="tpu_custom_call" | custom-call | tf_op jit(solution)/shard_map/spread/pallas_call | solution.py:365
  38.8 6.1 %all-to-all-start = ((f32[32,3,8,128]{3,2,1,0:T(8,128)}), f32[32,3,8,128]{3,2,1,0:T(8,128)S(1)}, u32[]{:S(2)}, u32[]{:S(2)}) async-start(f32[32,3,8,128]{3,2,1,0:T(8,128)} %spread.1), calls=%async_computation | async-start | bytes 786432 | tf_op jit(solution)/shard_map/all_to_all | solution.py:381
  45.6 7.9 %all-to-all-done.own_ref = f32[32,3,8,128]{3,2,1,0:T(8,128)S(1)} async-done(((f32[32,3,8,128]{3,2,1,0:T(8,128)}), f32[32,3,8,128]{3,2,1,0:T(8,128)S(1)}, u32[]{:S(2)}, u32[]{:S(2)}) %all-to-all-start) | async-done | bytes 393248 | tf_op jit(solution)/shard_map/all_to_all | solution.py:381
  53.5 1.9 %collective-permute-start.6 = (f32[32,3,8,128]{3,2,1,0:T(8,128)S(1)}, f32[32,3,8,128]{3,2,1,0:T(8,128)S(1)}, u32[]{:S(2)}, u32[]{:S(2)}) collective-permute-start(f32[32,3,8,128]{3,2,1,0:T(8,128)S(1)} %all-to-all-done.own_ref), channel_id=1, source_target_pairs={{0,1},{2,3},{4,5},{6,7},{8,9},{10,11},{12,13},{14,15},{1,0},{3,2},... | collective-permute-start | bytes 1179656 | tf_op jit(solution)/shard_map/ppermute | solution.py:384
  55.4 1.7 %collective-permute-done.6.other_ref = f32[32,3,8,128]{3,2,1,0:T(8,128)S(1)} collective-permute-done((f32[32,3,8,128]{3,2,1,0:T(8,128)S(1)}, f32[32,3,8,128]{3,2,1,0:T(8,128)S(1)}, u32[]{:S(2)}, u32[]{:S(2)}) %collective-permute-start.6) | collective-permute-done | bytes 393248 | tf_op jit(solution)/shard_map/ppermute | solution.py:384
  57.1 1.0 %wave.3 = f32[24,8,128]{2,1,0:T(8,128)S(1)} custom-call(f32[32,3,8,128]{3,2,1,0:T(8,128)S(1)} %all-to-all-done.own_ref, f32[32,3,8,128]{3,2,1,0:T(8,128)S(1)} %collective-permute-done.6.other_ref), custom_call_target="tpu_custom_call" | custom-call | tf_op jit(solution)/shard_map/wave/pallas_call | solution.py:396
  58.2 1.6 %collective-permute-start.8 = (f32[24,8,128]{2,1,0:T(8,128)S(1)}, f32[24,8,128]{2,1,0:T(8,128)S(1)}, u32[]{:S(2)}, u32[]{:S(2)}) collective-permute-start(f32[24,8,128]{2,1,0:T(8,128)S(1)} %wave.3), channel_id=1, source_target_pairs={{64,192},{66,194},{68,196},{70,198},{72,200},{74,202},{76,204},{78... | collective-permute-start | bytes 294920 | tf_op jit(solution)/shard_map/ppermute | solution.py:392
  59.7 1.3 %collective-permute-start.7 = (f32[24,8,128]{2,1,0:T(8,128)S(1)}, f32[24,8,128]{2,1,0:T(8,128)S(1)}, u32[]{:S(2)}, u32[]{:S(2)}) collective-permute-start(f32[24,8,128]{2,1,0:T(8,128)S(1)} %wave.3), channel_id=1, source_target_pairs={{64,128},{66,130},{68,132},{70,134},{72,136},{74,138},{76,140},{78... | collective-permute-start | bytes 294920 | tf_op jit(solution)/shard_map/ppermute | solution.py:393
  61.9 1.3 %collective-permute-done.7 = f32[24,8,128]{2,1,0:T(8,128)S(1)} collective-permute-done((f32[24,8,128]{2,1,0:T(8,128)S(1)}, f32[24,8,128]{2,1,0:T(8,128)S(1)}, u32[]{:S(2)}, u32[]{:S(2)}) %collective-permute-start.7) | collective-permute-done | bytes 98336 | tf_op jit(solution)/shard_map/ppermute | solution.py:393
  63.3 0.7 collective-permute-start.11
  64.0 0.7 collective-permute-start.10
  64.6 2.4 %collective-permute-start.9 = (f32[3,4,8,128]{3,2,1,0:T(8,128)S(1)}, f32[3,4,8,128]{3,2,1,0:T(8,128)S(1)}, u32[]{:S(2)}, u32[]{:S(2)}) collective-permute-start(f32[3,4,8,128]{3,2,1,0:T(8,128)S(1)} %get-tuple-element.31.end_ref), channel_id=1, source_target_pairs={{0,16},{16,32},{32,48},{48,64},{64,80},{80,96},{96,112},{128,144},... | collective-permute-start | bytes 147464 | tf_op jit(solution)/shard_map/ppermute | solution.py:428
  67.0 5.7 %collective-permute-done.9.prev_ref = f32[3,4,8,128]{3,2,1,0:T(8,128)S(1)} collective-permute-done((f32[3,4,8,128]{3,2,1,0:T(8,128)S(1)}, f32[3,4,8,128]{3,2,1,0:T(8,128)S(1)}, u32[]{:S(2)}, u32[]{:S(2)}) %collective-permute-start.9) | collective-permute-done | bytes 49184 | tf_op jit(solution)/shard_map/ppermute | solution.py:428
  72.8 0.7 collective-permute-start.12
  73.5 0.7 collective-permute-start.14
  74.9 1.6 %last.1 = f32[1,3,3,4,8,128]{5,4,3,2,1,0:T(8,128)} custom-call(f32[8,24,8,128]{3,2,1,0:T(8,128)S(1)} %unpack.1.base_ref, f32[24,8,128]{2,1,0:T(8,128)S(1)} %add.20.state_ref, f32[24,8,128]{2,1,0:T(8,128)S(1)} %collective-permute-done.13.given_ref, f32[24,8,128]{2,1,0:T(8,128)S(1)} %collective-permute-done.14.late_ref, f32[3,3,4,8,128]{4,3,2,1,0:T(8,128)S(1)} %bitcast.3, ...), custom_call_target="tpu_custom_call" | custom-call | tf_op jit(solution)/shard_map/last/pallas_call | solution.py:437
  (21 shorter events, 3.5 us)
Async XLA Ops:
  0.0 7.4 %copy-start = (f32[1,3,3,4,8,128]{5,4,3,2,1,0:T(8,128)S(1)}, f32[1,3,3,4,8,128]{5,4,3,2,1,0:T(8,128)}, u32[]{:S(2)}) copy-start(f32[1,3,3,4,8,128]{5,4,3,2,1,0:T(8,128)} %param.1) | copy-start | bytes 442372
  1.1 5.4 %collective-permute-start.1 = (f32[3,3,3,8,128]{4,3,2,1,0:T(8,128)S(1)}, f32[3,3,3,8,128]{4,3,2,1,0:T(8,128)S(1)}, u32[]{:S(2)}, u32[]{:S(2)}) collective-permute-start(f32[3,3,3,8,128]{4,3,2,1,0:T(8,128)S(1)} %get-tuple-element.43), channel_id=1, source_target_pairs={{1,2},{3,4},{5,6},{7,8},{9,10},{11,12},{13,14},{2,1},{4,3},{6,5},{... | collective-permute-start | bytes 331784 | tf_op jit(solution)/shard_map/ppermute | solution.py:352
  1.7 5.7 %collective-permute-start = (f32[3,3,3,8,128]{4,3,2,1,0:T(8,128)S(1)}, f32[3,3,3,8,128]{4,3,2,1,0:T(8,128)S(1)}, u32[]{:S(2)}, u32[]{:S(2)}) collective-permute-start(f32[3,3,3,8,128]{4,3,2,1,0:T(8,128)S(1)} %get-tuple-element.44), channel_id=1, source_target_pairs={{0,1},{2,3},{4,5},{6,7},{8,9},{10,11},{12,13},{14,15},{1,0},{3,2},... | collective-permute-start | bytes 331784 | tf_op jit(solution)/shard_map/ppermute | solution.py:353
  7.9 30.1 %collective-permute-start.2 = (f32[4,8,128]{2,1,0:T(8,128)S(1)}, f32[4,8,128]{2,1,0:T(8,128)S(1)}, u32[]{:S(2)}, u32[]{:S(2)}) collective-permute-start(f32[4,8,128]{2,1,0:T(8,128)S(1)} %get-tuple-element.24.own_ref), channel_id=1, source_target_pairs={{1,9},{2,10},{3,11},{4,12},{5,13},{6,14},{7,15},{8,0},{9,1},{10,2}... | collective-permute-start | bytes 49160 | tf_op jit(solution)/shard_map/ppermute | solution.py:362
  9.2 16.8 %collective-permute-start.3 = (f32[2,8,128]{2,1,0:T(8,128)S(1)}, f32[2,8,128]{2,1,0:T(8,128)S(1)}, u32[]{:S(2)}, u32[]{:S(2)}) collective-permute-start(f32[2,8,128]{2,1,0:T(8,128)S(1)} %get-tuple-element.25), channel_id=1, source_target_pairs={{0,9},{16,25},{32,41},{48,57},{64,73},{80,89},{96,105},{112,121},{... | collective-permute-start | bytes 24584 | tf_op jit(solution)/shard_map/ppermute | solution.py:363
  26.0 12.0 %collective-permute-start.4 = (f32[2,8,128]{2,1,0:T(8,128)S(1)}, f32[2,8,128]{2,1,0:T(8,128)S(1)}, u32[]{:S(2)}, u32[]{:S(2)}) collective-permute-start(f32[2,8,128]{2,1,0:T(8,128)S(1)} %collective-permute-done.3), channel_id=1, source_target_pairs={{9,8},{25,24},{41,40},{57,56},{73,72},{89,88},{105,104},{121,120},... | collective-permute-start | bytes 24584 | tf_op jit(solution)/shard_map/ppermute | solution.py:364
  38.8 14.7 %all-to-all-start = ((f32[32,3,8,128]{3,2,1,0:T(8,128)}), f32[32,3,8,128]{3,2,1,0:T(8,128)S(1)}, u32[]{:S(2)}, u32[]{:S(2)}) async-start(f32[32,3,8,128]{3,2,1,0:T(8,128)} %spread.1), calls=%async_computation | async-start | bytes 786432 | tf_op jit(solution)/shard_map/all_to_all | solution.py:381
  44.9 0.7 collective-permute-start.5
  53.5 3.6 %collective-permute-start.6 = (f32[32,3,8,128]{3,2,1,0:T(8,128)S(1)}, f32[32,3,8,128]{3,2,1,0:T(8,128)S(1)}, u32[]{:S(2)}, u32[]{:S(2)}) collective-permute-start(f32[32,3,8,128]{3,2,1,0:T(8,128)S(1)} %all-to-all-done.own_ref), channel_id=1, source_target_pairs={{0,1},{2,3},{4,5},{6,7},{8,9},{10,11},{12,13},{14,15},{1,0},{3,2},... | collective-permute-start | bytes 1179656 | tf_op jit(solution)/shard_map/ppermute | solution.py:384
  58.2 3.8 %collective-permute-start.8 = (f32[24,8,128]{2,1,0:T(8,128)S(1)}, f32[24,8,128]{2,1,0:T(8,128)S(1)}, u32[]{:S(2)}, u32[]{:S(2)}) collective-permute-start(f32[24,8,128]{2,1,0:T(8,128)S(1)} %wave.3), channel_id=1, source_target_pairs={{64,192},{66,194},{68,196},{70,198},{72,200},{74,202},{76,204},{78... | collective-permute-start | bytes 294920 | tf_op jit(solution)/shard_map/ppermute | solution.py:392
  59.7 3.5 %collective-permute-start.7 = (f32[24,8,128]{2,1,0:T(8,128)S(1)}, f32[24,8,128]{2,1,0:T(8,128)S(1)}, u32[]{:S(2)}, u32[]{:S(2)}) collective-permute-start(f32[24,8,128]{2,1,0:T(8,128)S(1)} %wave.3), channel_id=1, source_target_pairs={{64,128},{66,130},{68,132},{70,134},{72,136},{74,138},{76,140},{78... | collective-permute-start | bytes 294920 | tf_op jit(solution)/shard_map/ppermute | solution.py:393
  63.3 9.4 %collective-permute-start.11 = (f32[24,8,128]{2,1,0:T(8,128)S(1)}, f32[24,8,128]{2,1,0:T(8,128)S(1)}, u32[]{:S(2)}, u32[]{:S(2)}) collective-permute-start(f32[24,8,128]{2,1,0:T(8,128)S(1)} %wave.4), channel_id=1, source_target_pairs={{192,320},{194,322},{196,324},{198,326},{200,328},{202,330},{204,3... | collective-permute-start | bytes 294920 | tf_op jit(solution)/shard_map/ppermute | solution.py:392
  64.0 8.8 %collective-permute-start.10 = (f32[24,8,128]{2,1,0:T(8,128)S(1)}, f32[24,8,128]{2,1,0:T(8,128)S(1)}, u32[]{:S(2)}, u32[]{:S(2)}) collective-permute-start(f32[24,8,128]{2,1,0:T(8,128)S(1)} %wave.4), channel_id=1, source_target_pairs={{192,256},{194,258},{196,260},{198,262},{200,264},{202,266},{204,2... | collective-permute-start | bytes 294920 | tf_op jit(solution)/shard_map/ppermute | solution.py:393
  64.6 8.1 %collective-permute-start.9 = (f32[3,4,8,128]{3,2,1,0:T(8,128)S(1)}, f32[3,4,8,128]{3,2,1,0:T(8,128)S(1)}, u32[]{:S(2)}, u32[]{:S(2)}) collective-permute-start(f32[3,4,8,128]{3,2,1,0:T(8,128)S(1)} %get-tuple-element.31.end_ref), channel_id=1, source_target_pairs={{0,16},{16,32},{32,48},{48,64},{64,80},{80,96},{96,112},{128,144},... | collective-permute-start | bytes 147464 | tf_op jit(solution)/shard_map/ppermute | solution.py:428
  72.8 2.0 %collective-permute-start.12 = (f32[24,8,128]{2,1,0:T(8,128)S(1)}, f32[24,8,128]{2,1,0:T(8,128)S(1)}, u32[]{:S(2)}, u32[]{:S(2)}) collective-permute-start(f32[24,8,128]{2,1,0:T(8,128)S(1)} %wave.5), channel_id=1, source_target_pairs={{256,384},{258,386},{260,388},{262,390},{264,392},{266,394},{268,3... | collective-permute-start | bytes 294920 | tf_op jit(solution)/shard_map/ppermute | solution.py:434
  73.5 1.4 %collective-permute-start.14 = (f32[24,8,128]{2,1,0:T(8,128)S(1)}, f32[24,8,128]{2,1,0:T(8,128)S(1)}, u32[]{:S(2)}, u32[]{:S(2)}) collective-permute-start(f32[24,8,128]{2,1,0:T(8,128)S(1)} %wave.5), channel_id=1, source_target_pairs={{256,385},{258,387},{260,389},{262,391},{264,393},{266,395},{268,3... | collective-permute-start | bytes 294920 | tf_op jit(solution)/shard_map/ppermute | solution.py:435
  74.1 0.7 collective-permute-start.13

commit v4 on v2

--- a/solution.py
+++ b/solution.py
@@ -174,7 +174,7 @@
                 sent = []
                 for g in range(4):
                     slab = 4 * g + j
-                    at = i * 4 + (slab % 8) // 2, 2 if half else (slab // 8) ^ half_z
+                    at = (slab % 8) // 2 * 8 + i, 2 if half else (slab // 8) ^ half_z
                     if core is None:
                         sent.append(jnp.where(here % 2 == slab % 2, own_ref[at], other_ref[at]))
                     else:
@@ -371,7 +371,7 @@
 
     device = lambda zl, y, zh, x, core: (zl * 4 + y) * slabs + zh * 8 + x * 2 + core
     layers = [
-        [device(2 * g + zl, y, zh, x, core) for zl in range(2) for y in range(4) for x in range(4)]
+        [device(2 * g + zl, y, zh, x, core) for x in range(4) for zl in range(2) for y in range(4)]
         for g in range(GROUPS)
         for zh in range(2)
         for core in range(2)

time: 76.5 us -> 76.8 us (level)
  the two profiles are of different devices: /device:TPU:225 before, /device:TPU:105 now
where the time goes in v4:
time: 76.8 us; the launch traced here: 76.4 us
  starting transfers between devices  48.4 us (63%)
  waiting for transfers between devices  23.5 us (31%)
  Pallas kernels  3.22 us (4%)
  other arithmetic  1.09 us (1%)
    all_to_all x1, starting transfers between devices, local(): own = lax.all_to_all(copies, both, 0, 0, axis_index_groups=layers)  17.3 us
    ppermute x1, starting transfers between devices, local(): lax.ppermute(packed, 'space', [(i, (i + middle) % slabs) for i in range(1...  12.7 us
    ppermute x1, waiting for transfers between devices, local(): lax.ppermute(early, both, [(i, i + 1) for i in cores(range(1, GROUPS - 1))])  10.9 us
    all_to_all x1, waiting for transfers between devices, local(): own = lax.all_to_all(copies, both, 0, 0, axis_index_groups=layers)  6.73 us
    ppermute x1, starting transfers between devices, local(): lax.ppermute(own, 'space', swaps([(i, i + 1) for i in range(0, slabs, 2)]))  4.91 us
    ppermute x1, starting transfers between devices, local(): lax.ppermute(to_side, 'space', swaps([(i, i + 1) for i in range(1, slabs...  3.68 us
    ppermute x1, waiting for transfers between devices, local(): lax.ppermute(handed, 'tm', [(i, i + 1) for i in range(slices - 1) if i +...  3.2 us
    ppermute x1, starting transfers between devices, local(): lax.ppermute(jnp.where(even, top, bottom), 'space', swaps([(i, i + 1) for...  1.92 us
  transfers between devices with their start and end apart: 14, of which 6 were waited for; matrix products, arithmetic and copies ran while one was open for 0% of the time, Pallas kernels for 0%

profile of v4, /device:TPU:105, one launch (start us, length us, event | category | flops | bytes accessed | tf_op | source)
XLA Modules:
  0.0 76.4 jit_solution(5282581014375795260)
XLA Ops:
  0.0 1.1 %slice_select_fusion = (f32[3,3,3,8,128]{4,3,2,1,0:T(8,128)S(1)}, f32[3,3,3,8,128]{4,3,2,1,0:T(8,128)S(1)}) fusion(f32[3,3,4,8,128]{4,3,2,1,0:T(8,128)} %bitcast.1, pred[]{:T(512)S(6)} %eq.5), kind=kLoop, calls=%fused_computation | loop fusion | flops 55296 | bytes 442369 | tf_op jit(solution)/shard_map/jit(_where)/select_n | solution.py:349
  1.1 3.7 %collective-permute-start.1 = (f32[3,3,3,8,128]{4,3,2,1,0:T(8,128)S(1)}, f32[3,3,3,8,128]{4,3,2,1,0:T(8,128)S(1)}, u32[]{:S(2)}, u32[]{:S(2)}) collective-permute-start(f32[3,3,3,8,128]{4,3,2,1,0:T(8,128)S(1)} %get-tuple-element.41), channel_id=1, source_target_pairs={{1,2},{3,4},{5,6},{7,8},{9,10},{11,12},{13,14},{2,1},{4,3},{6,5},{... | collective-permute-start | bytes 331784 | tf_op jit(solution)/shard_map/ppermute | solution.py:350
  4.8 1.9 %collective-permute-start = (f32[3,3,3,8,128]{4,3,2,1,0:T(8,128)S(1)}, f32[3,3,3,8,128]{4,3,2,1,0:T(8,128)S(1)}, u32[]{:S(2)}, u32[]{:S(2)}) collective-permute-start(f32[3,3,3,8,128]{4,3,2,1,0:T(8,128)S(1)} %get-tuple-element.42), channel_id=1, source_target_pairs={{0,1},{2,3},{4,5},{6,7},{8,9},{10,11},{12,13},{14,15},{1,0},{3,2},... | collective-permute-start | bytes 331784 | tf_op jit(solution)/shard_map/ppermute | solution.py:351
  6.7 0.5 collective-permute-done.1.side_ref
  7.2 0.8 %collective-permute-done.near_ref = f32[3,3,3,8,128]{4,3,2,1,0:T(8,128)S(1)} collective-permute-done((f32[3,3,3,8,128]{4,3,2,1,0:T(8,128)S(1)}, f32[3,3,3,8,128]{4,3,2,1,0:T(8,128)S(1)}, u32[]{:S(2)}, u32[]{:S(2)}) %collective-permute-start) | collective-permute-done | bytes 110624 | tf_op jit(solution)/shard_map/ppermute | solution.py:351
  8.0 0.5 fine.1
  8.5 12.7 %collective-permute-start.2 = (f32[4,8,128]{2,1,0:T(8,128)S(1)}, f32[4,8,128]{2,1,0:T(8,128)S(1)}, u32[]{:S(2)}, u32[]{:S(2)}) collective-permute-start(f32[4,8,128]{2,1,0:T(8,128)S(1)} %get-tuple-element.23.own_ref), channel_id=1, source_target_pairs={{1,9},{2,10},{3,11},{4,12},{5,13},{6,14},{7,15},{8,0},{9,1},{10,2}... | collective-permute-start | bytes 49160 | tf_op jit(solution)/shard_map/ppermute | solution.py:360
  21.2 0.7 collective-permute-start.3
  21.9 0.7 collective-permute-start.4
  22.6 0.8 %spread.1 = f32[32,3,8,128]{3,2,1,0:T(8,128)} custom-call(f32[4,8,128]{2,1,0:T(8,128)S(1)} %get-tuple-element.23.own_ref, f32[4,8,128]{2,1,0:T(8,128)S(1)} %collective-permute-done.2.across_ref, f32[2,8,128]{2,1,0:T(8,128)S(1)} %collective-permute-done.4.passed_ref), custom_call_target="tpu_custom_call" | custom-call | tf_op jit(solution)/shard_map/spread/pallas_call | solution.py:363
  23.4 17.3 %all-to-all-start = ((f32[32,3,8,128]{3,2,1,0:T(8,128)}), f32[32,3,8,128]{3,2,1,0:T(8,128)S(1)}, u32[]{:S(2)}, u32[]{:S(2)}) async-start(f32[32,3,8,128]{3,2,1,0:T(8,128)} %spread.1), calls=%async_computation | async-start | bytes 786432 | tf_op jit(solution)/shard_map/all_to_all | solution.py:379
  40.6 0.7 collective-permute-start.5
  41.3 6.7 %all-to-all-done.own_ref = f32[32,3,8,128]{3,2,1,0:T(8,128)S(1)} async-done(((f32[32,3,8,128]{3,2,1,0:T(8,128)}), f32[32,3,8,128]{3,2,1,0:T(8,128)S(1)}, u32[]{:S(2)}, u32[]{:S(2)}) %all-to-all-start) | async-done | bytes 393248 | tf_op jit(solution)/shard_map/all_to_all | solution.py:379
  48.1 4.9 %collective-permute-start.6 = (f32[32,3,8,128]{3,2,1,0:T(8,128)S(1)}, f32[32,3,8,128]{3,2,1,0:T(8,128)S(1)}, u32[]{:S(2)}, u32[]{:S(2)}) collective-permute-start(f32[32,3,8,128]{3,2,1,0:T(8,128)S(1)} %all-to-all-done.own_ref), channel_id=1, source_target_pairs={{0,1},{2,3},{4,5},{6,7},{8,9},{10,11},{12,13},{14,15},{1,0},{3,2},... | collective-permute-start | bytes 1179656 | tf_op jit(solution)/shard_map/ppermute | solution.py:382
  53.0 1.3 %collective-permute-done.6.other_ref = f32[32,3,8,128]{3,2,1,0:T(8,128)S(1)} collective-permute-done((f32[32,3,8,128]{3,2,1,0:T(8,128)S(1)}, f32[32,3,8,128]{3,2,1,0:T(8,128)S(1)}, u32[]{:S(2)}, u32[]{:S(2)}) %collective-permute-start.6) | collective-permute-done | bytes 393248 | tf_op jit(solution)/shard_map/ppermute | solution.py:382
  54.3 0.7 collective-permute-start.7
  55.3 0.7 collective-permute-start.9
  56.0 1.9 %collective-permute-start.8 = (f32[3,4,8,128]{3,2,1,0:T(8,128)S(1)}, f32[3,4,8,128]{3,2,1,0:T(8,128)S(1)}, u32[]{:S(2)}, u32[]{:S(2)}) collective-permute-start(f32[3,4,8,128]{3,2,1,0:T(8,128)S(1)} %get-tuple-element.30.end_ref), channel_id=1, source_target_pairs={{0,16},{16,32},{32,48},{48,64},{64,80},{80,96},{96,112},{128,144},... | collective-permute-start | bytes 147464 | tf_op jit(solution)/shard_map/ppermute | solution.py:419
  57.9 3.2 %collective-permute-done.8.prev_ref = f32[3,4,8,128]{3,2,1,0:T(8,128)S(1)} collective-permute-done((f32[3,4,8,128]{3,2,1,0:T(8,128)S(1)}, f32[3,4,8,128]{3,2,1,0:T(8,128)S(1)}, u32[]{:S(2)}, u32[]{:S(2)}) %collective-permute-start.8) | collective-permute-done | bytes 49184 | tf_op jit(solution)/shard_map/ppermute | solution.py:419
  61.2 0.7 collective-permute-start.10
  61.8 0.7 collective-permute-start.12
  62.5 1.3 %collective-permute-start.11 = (f32[24,8,128]{2,1,0:T(8,128)S(1)}, f32[24,8,128]{2,1,0:T(8,128)S(1)}, u32[]{:S(2)}, u32[]{:S(2)}) collective-permute-start(f32[24,8,128]{2,1,0:T(8,128)S(1)} %add.11.state_ref), channel_id=1, source_target_pairs={{128,129},{130,131},{132,133},{134,135},{136,137},{138,139},{140,1... | collective-permute-start | bytes 294920 | tf_op jit(solution)/shard_map/ppermute | solution.py:425
  63.9 10.9 %collective-permute-done.11.given_ref = f32[24,8,128]{2,1,0:T(8,128)S(1)} collective-permute-done((f32[24,8,128]{2,1,0:T(8,128)S(1)}, f32[24,8,128]{2,1,0:T(8,128)S(1)}, u32[]{:S(2)}, u32[]{:S(2)}) %collective-permute-start.11) | collective-permute-done | bytes 98336 | tf_op jit(solution)/shard_map/ppermute | solution.py:425
  74.8 1.6 %last.1 = f32[1,3,3,4,8,128]{5,4,3,2,1,0:T(8,128)} custom-call(f32[8,24,8,128]{3,2,1,0:T(8,128)S(1)} %unpack.1.base_ref, f32[24,8,128]{2,1,0:T(8,128)S(1)} %add.12.state_ref, f32[24,8,128]{2,1,0:T(8,128)S(1)} %collective-permute-done.11.given_ref, f32[24,8,128]{2,1,0:T(8,128)S(1)} %collective-permute-done.12.late_ref, f32[3,3,4,8,128]{4,3,2,1,0:T(8,128)S(1)} %bitcast.3, ...), custom_call_target="tpu_custom_call" | custom-call | tf_op jit(solution)/shard_map/last/pallas_call | solution.py:426
  (16 shorter events, 0.4 us)
Async XLA Ops:
  0.0 8.0 %copy-start = (f32[1,3,3,4,8,128]{5,4,3,2,1,0:T(8,128)S(1)}, f32[1,3,3,4,8,128]{5,4,3,2,1,0:T(8,128)}, u32[]{:S(2)}) copy-start(f32[1,3,3,4,8,128]{5,4,3,2,1,0:T(8,128)} %param.1) | copy-start | bytes 442372
  1.1 6.1 %collective-permute-start.1 = (f32[3,3,3,8,128]{4,3,2,1,0:T(8,128)S(1)}, f32[3,3,3,8,128]{4,3,2,1,0:T(8,128)S(1)}, u32[]{:S(2)}, u32[]{:S(2)}) collective-permute-start(f32[3,3,3,8,128]{4,3,2,1,0:T(8,128)S(1)} %get-tuple-element.41), channel_id=1, source_target_pairs={{1,2},{3,4},{5,6},{7,8},{9,10},{11,12},{13,14},{2,1},{4,3},{6,5},{... | collective-permute-start | bytes 331784 | tf_op jit(solution)/shard_map/ppermute | solution.py:350
  4.8 3.2 %collective-permute-start = (f32[3,3,3,8,128]{4,3,2,1,0:T(8,128)S(1)}, f32[3,3,3,8,128]{4,3,2,1,0:T(8,128)S(1)}, u32[]{:S(2)}, u32[]{:S(2)}) collective-permute-start(f32[3,3,3,8,128]{4,3,2,1,0:T(8,128)S(1)} %get-tuple-element.42), channel_id=1, source_target_pairs={{0,1},{2,3},{4,5},{6,7},{8,9},{10,11},{12,13},{14,15},{1,0},{3,2},... | collective-permute-start | bytes 331784 | tf_op jit(solution)/shard_map/ppermute | solution.py:351
  8.5 14.1 %collective-permute-start.2 = (f32[4,8,128]{2,1,0:T(8,128)S(1)}, f32[4,8,128]{2,1,0:T(8,128)S(1)}, u32[]{:S(2)}, u32[]{:S(2)}) collective-permute-start(f32[4,8,128]{2,1,0:T(8,128)S(1)} %get-tuple-element.23.own_ref), channel_id=1, source_target_pairs={{1,9},{2,10},{3,11},{4,12},{5,13},{6,14},{7,15},{8,0},{9,1},{10,2}... | collective-permute-start | bytes 49160 | tf_op jit(solution)/shard_map/ppermute | solution.py:360
  21.2 0.7 collective-permute-start.3
  21.9 0.7 collective-permute-start.4
  23.4 24.7 %all-to-all-start = ((f32[32,3,8,128]{3,2,1,0:T(8,128)}), f32[32,3,8,128]{3,2,1,0:T(8,128)S(1)}, u32[]{:S(2)}, u32[]{:S(2)}) async-start(f32[32,3,8,128]{3,2,1,0:T(8,128)} %spread.1), calls=%async_computation | async-start | bytes 786432 | tf_op jit(solution)/shard_map/all_to_all | solution.py:379
  40.6 0.7 collective-permute-start.5
  48.1 6.2 %collective-permute-start.6 = (f32[32,3,8,128]{3,2,1,0:T(8,128)S(1)}, f32[32,3,8,128]{3,2,1,0:T(8,128)S(1)}, u32[]{:S(2)}, u32[]{:S(2)}) collective-permute-start(f32[32,3,8,128]{3,2,1,0:T(8,128)S(1)} %all-to-all-done.own_ref), channel_id=1, source_target_pairs={{0,1},{2,3},{4,5},{6,7},{8,9},{10,11},{12,13},{14,15},{1,0},{3,2},... | collective-permute-start | bytes 1179656 | tf_op jit(solution)/shard_map/ppermute | solution.py:382
  54.3 1.0 %collective-permute-start.7 = (f32[24,8,128]{2,1,0:T(8,128)S(1)}, f32[24,8,128]{2,1,0:T(8,128)S(1)}, u32[]{:S(2)}, u32[]{:S(2)}) collective-permute-start(f32[24,8,128]{2,1,0:T(8,128)S(1)} %wave.3), channel_id=1, source_target_pairs={{0,128},{2,130},{4,132},{6,134},{8,136},{10,138},{12,140},{14,142}... | collective-permute-start | bytes 294920 | tf_op jit(solution)/shard_map/ppermute | solution.py:406
  55.3 5.8 %collective-permute-start.9 = (f32[24,8,128]{2,1,0:T(8,128)S(1)}, f32[24,8,128]{2,1,0:T(8,128)S(1)}, u32[]{:S(2)}, u32[]{:S(2)}) collective-permute-start(f32[24,8,128]{2,1,0:T(8,128)S(1)} %wave.4), channel_id=1, source_target_pairs={{128,256},{130,258},{132,260},{134,262},{136,264},{138,266},{140,2... | collective-permute-start | bytes 294920 | tf_op jit(solution)/shard_map/ppermute | solution.py:420
  56.0 5.1 %collective-permute-start.8 = (f32[3,4,8,128]{3,2,1,0:T(8,128)S(1)}, f32[3,4,8,128]{3,2,1,0:T(8,128)S(1)}, u32[]{:S(2)}, u32[]{:S(2)}) collective-permute-start(f32[3,4,8,128]{3,2,1,0:T(8,128)S(1)} %get-tuple-element.30.end_ref), channel_id=1, source_target_pairs={{0,16},{16,32},{32,48},{48,64},{64,80},{80,96},{96,112},{128,144},... | collective-permute-start | bytes 147464 | tf_op jit(solution)/shard_map/ppermute | solution.py:419
  61.2 2.7 %collective-permute-start.10 = (f32[24,8,128]{2,1,0:T(8,128)S(1)}, f32[24,8,128]{2,1,0:T(8,128)S(1)}, u32[]{:S(2)}, u32[]{:S(2)}) collective-permute-start(f32[24,8,128]{2,1,0:T(8,128)S(1)} %wave.5), channel_id=1, source_target_pairs={{256,384},{258,386},{260,388},{262,390},{264,392},{266,394},{268,3... | collective-permute-start | bytes 294920 | tf_op jit(solution)/shard_map/ppermute | solution.py:420
  61.8 2.0 %collective-permute-start.12 = (f32[24,8,128]{2,1,0:T(8,128)S(1)}, f32[24,8,128]{2,1,0:T(8,128)S(1)}, u32[]{:S(2)}, u32[]{:S(2)}) collective-permute-start(f32[24,8,128]{2,1,0:T(8,128)S(1)} %wave.5), channel_id=1, source_target_pairs={{256,385},{258,387},{260,389},{262,391},{264,393},{266,395},{268,3... | collective-permute-start | bytes 294920 | tf_op jit(solution)/shard_map/ppermute | solution.py:424
  62.5 12.3 %collective-permute-start.11 = (f32[24,8,128]{2,1,0:T(8,128)S(1)}, f32[24,8,128]{2,1,0:T(8,128)S(1)}, u32[]{:S(2)}, u32[]{:S(2)}) collective-permute-start(f32[24,8,128]{2,1,0:T(8,128)S(1)} %add.11.state_ref), channel_id=1, source_target_pairs={{128,129},{130,131},{132,133},{134,135},{136,137},{138,139},{140,1... | collective-permute-start | bytes 294920 | tf_op jit(solution)/shard_map/ppermute | solution.py:425
